TPU v7x, 32 devices: a whole 2x2x4 slice. The times are simulated.
32 devices in a mesh: groups: 2 (over y), tp: 4 (over z), sec: 2 (over x), dp: 2 (over core).
Axes of the slice: x: 2, y: 2, z: 4, core: 2. Of those that a mesh axis runs over, the one named last changes fastest.
Arguments:
- giant_context: bfloat16 [6144, 2048], P('tp', ('groups', 'sec', 'dp')), parts along dimension 1, may hold values from -40 to 40
- clip_context: bfloat16 [5120, 2048], P('tp', ('groups', 'sec', 'dp')), parts along dimension 1, may hold values from -40 to 40
- giant_out: bfloat16 [6144, 6144], P('tp'), may hold values from -1 to 1
- clip_out: bfloat16 [5120, 5120], P('tp'), may hold values from -1 to 1
- giant_gain: float32 [6144], P('tp'), may hold values from 0.5 to 1.5
- clip_gain: float32 [5120], P('tp'), may hold values from 0.5 to 1.5
- student_features: bfloat16 [2048, 1280], P(('groups', 'sec', 'dp')), parts along dimension 0, may hold values from -6 to 6
- giant_first: bfloat16 [1280, 1280], P('tp'), may hold values from -0.15625 to 0.15625
- clip_first: bfloat16 [1280, 1280], P('tp'), may hold values from -0.15625 to 0.15625
- giant_head: bfloat16 [6144, 1280], P('tp'), may hold values from -2 to 2
- clip_head: bfloat16 [5120, 1280], P('tp'), may hold values from -2 to 2
Outputs:
- giant_grad: bfloat16 [12288, 1280], P(('groups', 'tp'), ('sec', 'dp')), parts along dimension 0
- clip_grad: bfloat16 [10240, 1280], P(('groups', 'tp'), ('sec', 'dp')), parts along dimension 0
- giant_first_grad: bfloat16 [2560, 1280], P(('groups', 'tp'), ('sec', 'dp')), parts along dimension 0
- clip_first_grad: bfloat16 [2560, 1280], P(('groups', 'tp'), ('sec', 'dp')), parts along dimension 0
- feature_grad: bfloat16 [2048, 1280], P(('groups', 'sec', 'dp')), parts along dimension 0
There are 2 independent parts, one for each index of `groups`. A program takes and returns all parts, laid end to end along the dimension named above; an argument that names none is the same for every part. Nothing has to cross between parts.
All inputs are finite; a program needn't handle non-finite values.
Results may differ from a plain program's by a relative error of at most 0.02.
Values may be sent and summed in bfloat16 or wider, within the bound.
A program may use at most 128 MiB of HBM per device.

v0:
```python
import math

import jax
import jax.numpy as jnp
from jax import lax
from jax.sharding import PartitionSpec as P

EPSILON = 1e-06
CONTRACT_FIRST = (((0,), (0,)), ((), ()))
CONTRACT_LAST = (((1,), (1,)), ((), ()))


def normal_cdf(values):
    return 0.5 * (1.0 + lax.erf(values * (1.0 / math.sqrt(2.0))))


def gelu_value(values):
    return values * normal_cdf(values)


def gelu_slope(values):
    return normal_cdf(values) + values * jnp.exp(-0.5 * values * values) * (
        1.0 / math.sqrt(2.0 * math.pi)
    )


def project_teacher(weight_rows, context):
    return lax.dot_general(weight_rows, context, CONTRACT_FIRST, preferred_element_type=jnp.float32)


def normalize(values, gain_rows, average, variance):
    inverse = lax.rsqrt(variance + EPSILON)
    return gain_rows[:, None] * (values - average) * inverse


def own_target(summed, gain_rows):
    share = gain_rows.shape[0]
    average = jnp.mean(summed, axis=0)
    variance = jnp.mean(summed * summed, axis=0) - average * average
    own_rows = lax.dynamic_slice_in_dim(summed, lax.axis_index("tp") * share, share, 0)
    return normalize(own_rows, gain_rows, average, variance)


def cosine_partials(predicted, target):
    return (
        jnp.sum(predicted * target, axis=0),
        jnp.sum(predicted * predicted, axis=0),
        jnp.sum(target * target, axis=0),
    )


def cosine_sums(giant_pred, giant_target, clip_pred, clip_target):
    return lax.psum(
        cosine_partials(giant_pred, giant_target) + cosine_partials(clip_pred, clip_target), "tp"
    )


def make_slope(predicted, target, inner, pred_sq, target_sq, width):
    inv_pred = lax.rsqrt(pred_sq + EPSILON)
    inv_target = lax.rsqrt(target_sq + EPSILON)
    cosine = inner * inv_pred * inv_target
    weight = width / 8.0
    slope = -weight * (
        target * (inv_pred * inv_target) - predicted * (cosine * inv_pred * inv_pred)
    )
    return slope.astype(jnp.bfloat16)


def local(
    giant_context,
    clip_context,
    giant_out,
    clip_out,
    giant_gain,
    clip_gain,
    student_features,
    giant_first,
    clip_first,
    giant_head,
    clip_head,
):
    giant_width = giant_out.shape[1]
    clip_width = clip_out.shape[1]
    giant_pre = lax.dot_general(
        student_features, giant_first, CONTRACT_LAST, preferred_element_type=jnp.float32
    )
    clip_pre = lax.dot_general(
        student_features, clip_first, CONTRACT_LAST, preferred_element_type=jnp.float32
    )
    giant_hidden_own = gelu_value(giant_pre).astype(jnp.bfloat16)
    clip_hidden_own = gelu_value(clip_pre).astype(jnp.bfloat16)
    giant_hidden, clip_hidden = (
        lax.all_gather(giant_hidden_own, "tp", axis=1, tiled=True),
        lax.all_gather(clip_hidden_own, "tp", axis=1, tiled=True),
    )
    giant_pred = lax.dot_general(
        giant_head, giant_hidden, CONTRACT_LAST, preferred_element_type=jnp.float32
    )
    clip_pred = lax.dot_general(
        clip_head, clip_hidden, CONTRACT_LAST, preferred_element_type=jnp.float32
    )
    giant_full = lax.psum(
        project_teacher(giant_out, giant_context).astype(jnp.bfloat16), "tp"
    ).astype(jnp.float32)
    giant_target = own_target(giant_full, giant_gain)
    clip_full = lax.psum(project_teacher(clip_out, clip_context).astype(jnp.bfloat16), "tp").astype(
        jnp.float32
    )
    clip_target = own_target(clip_full, clip_gain)
    sums = cosine_sums(giant_pred, giant_target, clip_pred, clip_target)
    giant_stats = sums[0:3]
    clip_stats = sums[3:6]
    giant_slope = make_slope(
        giant_pred, giant_target, giant_stats[0], giant_stats[1], giant_stats[2], giant_width
    )
    clip_slope = make_slope(
        clip_pred, clip_target, clip_stats[0], clip_stats[1], clip_stats[2], clip_width
    )
    giant_second = jnp.dot(giant_slope, giant_hidden, preferred_element_type=jnp.float32)
    clip_second = jnp.dot(clip_slope, clip_hidden, preferred_element_type=jnp.float32)
    giant_hslope = lax.psum_scatter(
        lax.dot_general(
            giant_head, giant_slope, CONTRACT_FIRST, preferred_element_type=jnp.float32
        ).astype(jnp.bfloat16),
        "tp",
        scatter_dimension=0,
        tiled=True,
    ).astype(jnp.float32)
    clip_hslope = lax.psum_scatter(
        lax.dot_general(
            clip_head, clip_slope, CONTRACT_FIRST, preferred_element_type=jnp.float32
        ).astype(jnp.bfloat16),
        "tp",
        scatter_dimension=0,
        tiled=True,
    ).astype(jnp.float32)
    giant_pslope = (giant_hslope * gelu_slope(giant_pre.T)).astype(jnp.bfloat16)
    clip_pslope = (clip_hslope * gelu_slope(clip_pre.T)).astype(jnp.bfloat16)
    giant_one = jnp.dot(giant_pslope, student_features, preferred_element_type=jnp.float32)
    clip_one = jnp.dot(clip_pslope, student_features, preferred_element_type=jnp.float32)
    feature_term = lax.dot_general(
        giant_pslope, giant_first, CONTRACT_FIRST, preferred_element_type=jnp.float32
    )
    feature_term = feature_term + lax.dot_general(
        clip_pslope, clip_first, CONTRACT_FIRST, preferred_element_type=jnp.float32
    )
    feature_sum = lax.psum(feature_term.astype(jnp.bfloat16), "tp")
    giant_grad, clip_grad, giant_first_grad, clip_first_grad = (
        lax.psum_scatter(
            giant_second.astype(jnp.bfloat16), ("sec", "dp"), scatter_dimension=1, tiled=True
        ).astype(jnp.float32),
        lax.psum_scatter(
            clip_second.astype(jnp.bfloat16), ("sec", "dp"), scatter_dimension=1, tiled=True
        ).astype(jnp.float32),
        lax.psum_scatter(
            giant_one.astype(jnp.bfloat16), ("sec", "dp"), scatter_dimension=1, tiled=True
        ).astype(jnp.float32),
        lax.psum_scatter(
            clip_one.astype(jnp.bfloat16), ("sec", "dp"), scatter_dimension=1, tiled=True
        ).astype(jnp.float32),
    )
    return (
        giant_grad.astype(jnp.bfloat16),
        clip_grad.astype(jnp.bfloat16),
        giant_first_grad.astype(jnp.bfloat16),
        clip_first_grad.astype(jnp.bfloat16),
        feature_sum,
    )


def solution(mesh):
    placed = (
        P("tp", ("groups", "sec", "dp")),
        P("tp", ("groups", "sec", "dp")),
        P("tp", None),
        P("tp", None),
        P("tp"),
        P("tp"),
        P(("groups", "sec", "dp"), None),
        P("tp", None),
        P("tp", None),
        P("tp", None),
        P("tp", None),
    )
    return jax.shard_map(
        local,
        mesh=mesh,
        in_specs=placed,
        out_specs=(
            P(("groups", "tp"), ("sec", "dp")),
            P(("groups", "tp"), ("sec", "dp")),
            P(("groups", "tp"), ("sec", "dp")),
            P(("groups", "tp"), ("sec", "dp")),
            P(("groups", "sec", "dp"), None),
        ),
        check_vma=False,
    )
```

profile of v0, /device:TPU:0, one launch (start us, length us, event | category | flops | bytes accessed | tf_op | source)
XLA Modules:
  0.0 518.6 jit_solution(12912610916544960796)
XLA Ops:
  7.2 0.0 copy-start
  7.2 0.0 all-reduce.7.cloned.1.call-start
  7.2 10.8 %convolution_convert_fusion = bf16[6144,256]{1,0:T(8,128)(2,1)} fusion(bf16[1536,6144]{1,0:T(8,128)(2,1)} %param.13, bf16[1536,256]{1,0:T(8,128)(2,1)} %param.11), kind=kOutput, calls=%fused_computation | convolution fusion | flops 4833411072 | bytes 22806528 | tf_op jit(solution)/shard_map/dot_general | solution.py:28
  18.0 0.8 copy-done.16
  18.8 0.1 copy-done.19
  18.9 5.2 %convolution_convert_fusion.3 = bf16[5120,256]{1,0:T(8,128)(2,1)} fusion(bf16[1280,5120]{1,0:T(8,128)(2,1)S(1)} %copy-done.16, bf16[1280,256]{1,0:T(8,128)(2,1)S(1)} %copy-done.19), kind=kOutput, calls=%fused_computation.3 | convolution fusion | flops 3356753920 | bytes 16384000 | tf_op jit(solution)/shard_map/dot_general | solution.py:28
  24.1 0.0 all-reduce.7.cloned.1.call-update
  24.2 0.0 reduce-scatter.17.cloned.1.call-start
  24.2 0.0 copy-start.8
  24.2 2.6 multiply_convert_fusion.2
  26.9 27.7 %all_gather.7 = bf16[256,1280]{0,1:T(8,128)(2,1)} all-gather(bf16[256,320]{0,1:T(8,128)(2,1)S(1)} %get-tuple-element.34), channel_id=1, replica_groups=mesh['groups'=2,'tp'=4,'sec'=2,'dp'=2] {'tp'}, dimensions={1}, use_global_device_ids=true | all-gather | bytes 819200 | tf_op jit(solution)/shard_map/all_gather | solution.py:94
  54.6 1.2 multiply_convert_fusion.3
  55.7 26.7 %all_gather.6 = bf16[256,1280]{0,1:T(8,128)(2,1)} all-gather(bf16[256,320]{0,1:T(8,128)(2,1)S(1)} %get-tuple-element.31), channel_id=1, replica_groups=mesh['groups'=2,'tp'=4,'sec'=2,'dp'=2] {'tp'}, dimensions={1}, use_global_device_ids=true | all-gather | bytes 819200 | tf_op jit(solution)/shard_map/all_gather | solution.py:93
  82.4 170.1 %all-reduce.7.cloned.1.call-done = (bf16[6144,256]{1,0:T(8,128)(2,1)}, bf16[5120,256]{1,0:T(8,128)(2,1)}) async-done(((bf16[6144,256]{1,0:T(8,128)(2,1)}, bf16[5120,256]{1,0:T(8,128)(2,1)}), (bf16[6144,256]{1,0:T(8,128)(2,1)}, bf16[5120,256]{1,0:T(8,128)(2,1)})) %all-reduce.7.cloned.1.call-update) | async-done | bytes 5767184 | tf_op jit(solution)/shard_map/psum | solution.py:102
  252.5 2.6 convert_reduce_fusion.1
  255.1 0.4 convert_element_type.77
  255.6 2.7 copy-done.1
  258.3 0.9 convert_reduce_fusion
  259.1 0.0 copy-start.14
  259.1 0.5 convert_element_type.72
  259.7 0.5 copy-done.12
  260.2 2.2 multiply_reduce_fusion.6
  262.4 0.8 copy-done.4
  263.2 1.5 copy-done.17
  264.6 2.6 multiply_reduce_fusion.3
  267.2 9.7 %all-reduce = (f32[256]{0:T(256)S(1)}, f32[256]{0:T(256)S(1)}, f32[256]{0:T(256)S(1)}, f32[256]{0:T(256)S(1)}, f32[256]{0:T(256)S(1)}, /*index=5*/f32[256]{0:T(256)S(1)}) all-reduce(f32[256]{0:T(256)S(1)} %get-tuple-element.6, f32[256]{0:T(256)S(1)} %get-tuple-element.13, ...), channel_id=1, replica_groups=mesh['groups'=2,'tp'=4,'sec'=2,'dp'=2] {'tp'}, use_global_device_ids=true, to_apply=%region_8.0 | all-reduce | flops 1536 | bytes 12288 | tf_op jit(solution)/shard_map/psum | solution.py:53
  276.9 2.1 multiply_convert_fusion.1
  279.0 0.8 copy-done.7
  279.8 2.2 fusion.2
  282.1 0.0 reduce-scatter.17.cloned.1.call-update
  282.1 0.0 reduce-scatter.15.cloned.1.call-start
  282.2 2.5 multiply_convert_fusion
  284.7 0.0 copy-start.6
  284.7 0.9 copy-done.6
  285.5 2.6 fusion.1
  288.1 0.0 reduce-scatter.15.cloned.1.call-update
  288.2 0.0 reduce-scatter.21.cloned.1.call-start
  288.2 14.8 %reduce-scatter.17.cloned.1.call-done = bf16[320,256]{1,0:T(8,128)(2,1)} async-done(((bf16[1280,256]{1,0:T(8,128)(2,1)}), bf16[320,256]{1,0:T(8,128)(2,1)}) %reduce-scatter.17.cloned.1.call-update) | async-done | bytes 163856 | tf_op jit(solution)/shard_map/reduce_scatter | solution.py:129
  303.0 2.6 convolution_convert_fusion.4
  305.7 2.2 copy.30
  307.9 0.0 reduce-scatter.21.cloned.1.call-update
  307.9 0.0 reduce-scatter.19.cloned.1.call-start
  307.9 18.5 %reduce-scatter.15.cloned.1.call-done = bf16[320,256]{1,0:T(8,128)(2,1)} async-done(((bf16[1280,256]{1,0:T(8,128)(2,1)}), bf16[320,256]{1,0:T(8,128)(2,1)}) %reduce-scatter.15.cloned.1.call-update) | async-done | bytes 163856 | tf_op jit(solution)/shard_map/reduce_scatter | solution.py:121
  326.4 2.6 convolution_convert_fusion.5
  329.1 2.2 copy.28
  331.3 0.0 reduce-scatter.19.cloned.1.call-update
  331.3 0.0 all-reduce.5.cloned.1.call-start
  331.4 2.0 fusion.25
  333.5 1.5 fusion
  334.9 0.0 all-reduce.5.cloned.1.call-update
  334.9 0.0 reduce-scatter.13.cloned.1.call-start
  335.0 4.1 convolution_convert_fusion.1
  339.1 0.0 reduce-scatter.13.cloned.1.call-update
  339.1 0.0 reduce-scatter.11.cloned.1.call-start
  339.2 4.4 convolution_convert_fusion.2
  343.6 0.0 reduce-scatter.11.cloned.1.call-update
  343.6 8.6 %reduce-scatter.21.cloned.1.call-done = bf16[320,320]{1,0:T(8,128)(2,1)} async-done(((bf16[1280,320]{1,0:T(8,128)(2,1)}), bf16[320,320]{1,0:T(8,128)(2,1)}) %reduce-scatter.21.cloned.1.call-update) | async-done | bytes 204816
  352.3 1.8 copy.31
  354.1 25.3 %reduce-scatter.19.cloned.1.call-done = bf16[320,320]{1,0:T(8,128)(2,1)} async-done(((bf16[1280,320]{1,0:T(8,128)(2,1)}), bf16[320,320]{1,0:T(8,128)(2,1)}) %reduce-scatter.19.cloned.1.call-update) | async-done | bytes 204816
  379.4 1.8 copy.29
  381.2 40.9 %all-reduce.5.cloned.1.call-done = bf16[256,1280]{1,0:T(8,128)(2,1)} async-done(((bf16[256,1280]{1,0:T(8,128)(2,1)}), bf16[256,1280]{1,0:T(8,128)(2,1)}) %all-reduce.5.cloned.1.call-update) | async-done | bytes 655376 | tf_op jit(solution)/shard_map/psum | solution.py:147
  422.1 41.4 %reduce-scatter.13.cloned.1.call-done = bf16[1280,320]{0,1:T(8,128)(2,1)} async-done(((bf16[1280,1280]{0,1:T(8,128)(2,1)}), bf16[1280,320]{0,1:T(8,128)(2,1)}) %reduce-scatter.13.cloned.1.call-update) | async-done | bytes 819216 | tf_op jit(solution)/shard_map/reduce_scatter | solution.py:152
  463.5 46.2 %reduce-scatter.11.cloned.1.call-done = bf16[1536,320]{0,1:T(8,128)(2,1)} async-done(((bf16[1536,1280]{0,1:T(8,128)(2,1)}), bf16[1536,320]{0,1:T(8,128)(2,1)}) %reduce-scatter.11.cloned.1.call-update) | async-done | bytes 983056 | tf_op jit(solution)/shard_map/reduce_scatter | solution.py:149
  509.8 2.0 copy.35
  (31 shorter events, 0.1 us)
Async XLA Ops:
  7.2 252.5 %copy-start = (bf16[1280,1280]{1,0:T(8,128)(2,1)S(1)}, bf16[1280,1280]{1,0:T(8,128)(2,1)}, u32[]{:S(2)}) copy-start(bf16[1280,1280]{1,0:T(8,128)(2,1)} %param.21) | copy-start | bytes 9830404
  7.2 245.3 %all-reduce.7.cloned.1.call-start = ((), (), s32[]{:S(2)}) async-start(), calls=%async_computation.13 | async-start | bytes 11534336 | tf_op jit(solution)/shard_map/psum | solution.py:102
  7.2 11.6 %copy-start.16 = (bf16[1280,5120]{1,0:T(8,128)(2,1)S(1)}, bf16[1280,5120]{1,0:T(8,128)(2,1)}, u32[]{:S(2)}) copy-start(bf16[1280,5120]{1,0:T(8,128)(2,1)} %param.14) | copy-start | bytes 39321604
  7.2 11.7 %copy-start.19 = (bf16[1280,256]{1,0:T(8,128)(2,1)S(1)}, bf16[1280,256]{1,0:T(8,128)(2,1)}, u32[]{:S(2)}) copy-start(bf16[1280,256]{1,0:T(8,128)(2,1)} %param.12) | copy-start | bytes 1966084
  24.2 278.9 %reduce-scatter.17.cloned.1.call-start = ((), (), s32[]{:S(2)}) async-start(), calls=%async_computation.9 | async-start | bytes 819200 | tf_op jit(solution)/shard_map/reduce_scatter | solution.py:129
  24.2 30.3 %copy-start.3 = (bf16[256,1280]{1,0:T(8,128)(2,1)S(1)}, bf16[256,1280]{1,0:T(8,128)(2,1)}, u32[]{:S(2)}) copy-start(bf16[256,1280]{1,0:T(8,128)(2,1)} %param.17) | copy-start | bytes 1966084
  24.2 30.3 %copy-start.8 = (bf16[320,1280]{1,0:T(8,128)(2,1)S(1)}, bf16[320,1280]{1,0:T(8,128)(2,1)}, u32[]{:S(2)}) copy-start(bf16[320,1280]{1,0:T(8,128)(2,1)} %param.18) | copy-start | bytes 2457604
  252.5 2.6 copy-start.2
  255.1 3.1 copy-start.1
  255.5 4.1 copy-start.5
  259.1 1.1 copy-start.12
  259.1 1.1 copy-start.14
  259.6 3.5 copy-start.4
  260.2 3.0 copy-start.11
  260.2 3.0 copy-start.15
  260.2 4.4 copy-start.17
  279.0 0.8 copy-start.7
  282.1 44.3 %reduce-scatter.15.cloned.1.call-start = ((), (), s32[]{:S(2)}) async-start(), calls=%async_computation.8 | async-start | bytes 819200 | tf_op jit(solution)/shard_map/reduce_scatter | solution.py:121
  282.2 3.4 copy-start.18
  284.7 0.9 copy-start.6
  288.2 64.1 %reduce-scatter.21.cloned.1.call-start = ((), (), s32[]{:S(2)}) async-start(), calls=%async_computation.12 | async-start | bytes 1228800
  307.9 71.5 %reduce-scatter.19.cloned.1.call-start = ((), (), s32[]{:S(2)}) async-start(), calls=%async_computation.11 | async-start | bytes 1228800
  331.3 2.1 copy-start.13
  331.3 90.8 %all-reduce.5.cloned.1.call-start = ((), (), s32[]{:S(2)}) async-start(), calls=%async_computation.10 | async-start | bytes 1310720 | tf_op jit(solution)/shard_map/psum | solution.py:147
  331.4 2.1 copy-start.9
  331.4 2.1 copy-start.10
  334.9 128.6 %reduce-scatter.13.cloned.1.call-start = ((), (), s32[]{:S(2)}) async-start(), calls=%async_computation.7 | async-start | bytes 4096000 | tf_op jit(solution)/shard_map/reduce_scatter | solution.py:152
  339.1 170.6 %reduce-scatter.11.cloned.1.call-start = ((), (), s32[]{:S(2)}) async-start(), calls=%async_computation.6 | async-start | bytes 4915200 | tf_op jit(solution)/shard_map/reduce_scatter | solution.py:149
Sparse Core Ops, SparseCore 0:
  24.3 228.1 all-reduce.6
  282.2 20.7 reduce-scatter.16
  305.3 21.0 reduce-scatter.14
  328.9 23.3 reduce-scatter.20
  354.9 24.4 reduce-scatter.18
  381.6 40.4 all-reduce.4
  425.3 38.2 reduce-scatter.12
  466.8 42.8 reduce-scatter.10
where the time goes:
time: 519 us
  waiting for transfers between devices  366 us (71%)
  blocking collectives  64 us (12%)
  matrix products  46.6 us (9%)
  local copies, waits for them, and re-layouts  18.1 us (3%)
  between operations  14.4 us (3%)
  other arithmetic  8.97 us (2%)
    psum x1, waiting for transfers between devices, local(): lax.psum(project_teacher(giant_out, giant_context).astype(jnp.bfloat16),...  170 us
    reduce_scatter x1, waiting for transfers between devices, local(): lax.psum_scatter(giant_second.astype(jnp.bfloat16), ('sec', 'dp'), scatte...  46.2 us
    reduce_scatter x1, waiting for transfers between devices, local(): lax.psum_scatter(clip_second.astype(jnp.bfloat16), ('sec', 'dp'), scatter...  41.4 us
    psum x1, waiting for transfers between devices, local(): feature_sum = lax.psum(feature_term.astype(jnp.bfloat16), 'tp')  40.9 us
    unnamed x10, waiting for transfers between devices  34.1 us
    all_gather x1, blocking collectives, local(): lax.all_gather(clip_hidden_own, 'tp', axis=1, tiled=True)  27.7 us
    all_gather x1, blocking collectives, local(): lax.all_gather(giant_hidden_own, 'tp', axis=1, tiled=True)  26.7 us
    reduce_scatter x1, waiting for transfers between devices, local(): lax.psum_scatter(lax.dot_general(giant_head, giant_slope, CONTRACT_FIRST,...  18.5 us
  transfers between devices with their start and end apart: 8, of which 8 were waited for; matrix products, arithmetic and copies ran while one was open for 7% of the time, Pallas kernels for 0%

commit v1 on v0

--- a/solution.py
+++ b/solution.py
@@ -28,38 +28,36 @@
     return lax.dot_general(weight_rows, context, CONTRACT_FIRST, preferred_element_type=jnp.float32)
 
 
-def normalize(values, gain_rows, average, variance):
-    inverse = lax.rsqrt(variance + EPSILON)
-    return gain_rows[:, None] * (values - average) * inverse
-
-
-def own_target(summed, gain_rows):
-    share = gain_rows.shape[0]
-    average = jnp.mean(summed, axis=0)
-    variance = jnp.mean(summed * summed, axis=0) - average * average
-    own_rows = lax.dynamic_slice_in_dim(summed, lax.axis_index("tp") * share, share, 0)
-    return normalize(own_rows, gain_rows, average, variance)
-
-
-def cosine_partials(predicted, target):
-    return (
-        jnp.sum(predicted * target, axis=0),
-        jnp.sum(predicted * predicted, axis=0),
-        jnp.sum(target * target, axis=0),
+def token_sums(own, gain_rows, predicted):
+    gain = gain_rows[:, None]
+    scaled = gain * own
+    return jnp.stack(
+        (
+            jnp.sum(own, axis=0),
+            jnp.sum(own * own, axis=0),
+            jnp.sum(predicted * predicted, axis=0),
+            jnp.sum(scaled * predicted, axis=0),
+            jnp.sum(gain * predicted, axis=0),
+            jnp.sum(scaled * scaled, axis=0),
+            jnp.sum(gain * scaled, axis=0),
+            jnp.broadcast_to(jnp.sum(gain * gain), own.shape[1:]),
+        )
     )
 
 
-def cosine_sums(giant_pred, giant_target, clip_pred, clip_target):
-    return lax.psum(
-        cosine_partials(giant_pred, giant_target) + cosine_partials(clip_pred, clip_target), "tp"
+def make_slope(own, gain_rows, predicted, sums, width):
+    average = sums[0] / width
+    inverse = lax.rsqrt(sums[1] / width - average * average + EPSILON)
+    pred_sq = sums[2]
+    inner = inverse * (sums[3] - average * sums[4])
+    target_sq = inverse * inverse * (
+        sums[5] - 2.0 * average * sums[6] + average * average * sums[7]
     )
-
-
-def make_slope(predicted, target, inner, pred_sq, target_sq, width):
     inv_pred = lax.rsqrt(pred_sq + EPSILON)
     inv_target = lax.rsqrt(target_sq + EPSILON)
     cosine = inner * inv_pred * inv_target
     weight = width / 8.0
+    target = gain_rows[:, None] * (own - average) * inverse
     slope = -weight * (
         target * (inv_pred * inv_target) - predicted * (cosine * inv_pred * inv_pred)
     )
@@ -99,23 +97,27 @@
     clip_pred = lax.dot_general(
         clip_head, clip_hidden, CONTRACT_LAST, preferred_element_type=jnp.float32
     )
-    giant_full = lax.psum(
-        project_teacher(giant_out, giant_context).astype(jnp.bfloat16), "tp"
+    giant_own = lax.psum_scatter(
+        project_teacher(giant_out, giant_context).astype(jnp.bfloat16),
+        "tp",
+        scatter_dimension=0,
+        tiled=True,
     ).astype(jnp.float32)
-    giant_target = own_target(giant_full, giant_gain)
-    clip_full = lax.psum(project_teacher(clip_out, clip_context).astype(jnp.bfloat16), "tp").astype(
-        jnp.float32
+    clip_own = lax.psum_scatter(
+        project_teacher(clip_out, clip_context).astype(jnp.bfloat16),
+        "tp",
+        scatter_dimension=0,
+        tiled=True,
+    ).astype(jnp.float32)
+    giant_stats, clip_stats = lax.psum(
+        (
+            token_sums(giant_own, giant_gain, giant_pred),
+            token_sums(clip_own, clip_gain, clip_pred),
+        ),
+        "tp",
     )
-    clip_target = own_target(clip_full, clip_gain)
-    sums = cosine_sums(giant_pred, giant_target, clip_pred, clip_target)
-    giant_stats = sums[0:3]
-    clip_stats = sums[3:6]
-    giant_slope = make_slope(
-        giant_pred, giant_target, giant_stats[0], giant_stats[1], giant_stats[2], giant_width
-    )
-    clip_slope = make_slope(
-        clip_pred, clip_target, clip_stats[0], clip_stats[1], clip_stats[2], clip_width
-    )
+    giant_slope = make_slope(giant_own, giant_gain, giant_pred, giant_stats, giant_width)
+    clip_slope = make_slope(clip_own, clip_gain, clip_pred, clip_stats, clip_width)
     giant_second = jnp.dot(giant_slope, giant_hidden, preferred_element_type=jnp.float32)
     clip_second = jnp.dot(clip_slope, clip_hidden, preferred_element_type=jnp.float32)
     giant_hslope = lax.psum_scatter(

time: 519 us -> 421 us (0.81)
  waiting for transfers between devices: 366 us -> 256 us
  matrix products: 46.6 us -> 57.8 us
  blocking collectives: 64 us -> 72.4 us
    psum x1 -> x0, waiting for transfers between devices: 170 us -> none  [local(): lax.psum(project_teacher(giant_out, giant_context).astype(jnp.bfloat16),...]
    reduce_scatter x0 -> x2, waiting for transfers between devices: none -> 62.5 us  [the longest x1 57.9 us: local(): lax.psum_scatter(project_teacher(giant_out, giant_context).astype(jnp.bfl...]
    psum x1, blocking collectives: 9.68 us -> 17.5 us  [local(): lax.psum((token_sums(giant_own, giant_gain, giant_pred), token_sums(clip_...]
    unnamed x45 -> x25, local copies, waits for them, and re-layouts: 18.1 us -> 12.4 us
    unnamed x10 -> x11, waiting for transfers between devices: 34.1 us -> 34.1 us
  transfers between devices with their start and end apart: 8 -> 9, of which waited for: 8 -> 9; matrix products, arithmetic and copies ran while one was open for 7% -> 12% of each run, Pallas kernels for 0% -> 0%
where the time goes in v1:
time: 421 us; the launch traced here: 420 us
  waiting for transfers between devices  256 us (61%)
  blocking collectives  72.4 us (17%)
  matrix products  57.8 us (14%)
  between operations  14 us (3%)
  local copies, waits for them, and re-layouts  13.7 us (3%)
  other arithmetic  5.31 us (1%)
    reduce_scatter x1, waiting for transfers between devices, local(): lax.psum_scatter(project_teacher(giant_out, giant_context).astype(jnp.bfl...  57.9 us
    reduce_scatter x1, waiting for transfers between devices, local(): lax.psum_scatter(giant_second.astype(jnp.bfloat16), ('sec', 'dp'), scatte...  46.2 us
    reduce_scatter x1, waiting for transfers between devices, local(): lax.psum_scatter(clip_second.astype(jnp.bfloat16), ('sec', 'dp'), scatter...  41.4 us
    psum x1, waiting for transfers between devices, local(): feature_sum = lax.psum(feature_term.astype(jnp.bfloat16), 'tp')  41.1 us
    unnamed x11, waiting for transfers between devices  34.1 us
    all_gather x1, blocking collectives, local(): lax.all_gather(clip_hidden_own, 'tp', axis=1, tiled=True)  28 us
    all_gather x1, blocking collectives, local(): lax.all_gather(giant_hidden_own, 'tp', axis=1, tiled=True)  26.9 us
    dot_general x2, matrix products, project_teacher(): lax.dot_general(weight_rows, context, CONTRACT_FIRST, preferred_element_t...  20.8 us
  transfers between devices with their start and end apart: 9, of which 9 were waited for; matrix products, arithmetic and copies ran while one was open for 12% of the time, Pallas kernels for 0%

profile of v1, /device:TPU:0, one launch (start us, length us, event | category | flops | bytes accessed | tf_op | source)
XLA Modules:
  0.0 420.0 jit_solution(13595789393246182965)
XLA Ops:
  7.2 0.0 copy-start
  7.2 0.0 reduce-scatter.17.cloned.1.call-start
  7.2 10.2 %convolution_convert_fusion.3 = bf16[5120,256]{1,0:T(8,128)(2,1)} fusion(bf16[1280,5120]{1,0:T(8,128)(2,1)} %param.14, bf16[1280,256]{1,0:T(8,128)(2,1)} %param.12), kind=kOutput, calls=%fused_computation.3 | convolution fusion | flops 3356753920 | bytes 16384000 | tf_op jit(solution)/shard_map/dot_general | solution.py:28
  17.5 0.0 reduce-scatter.17.cloned.1.call-update
  17.5 0.0 reduce-scatter.13.cloned.1.call-start
  17.5 10.6 %convolution_convert_fusion = bf16[6144,256]{1,0:T(8,128)(2,1)} fusion(bf16[1536,6144]{1,0:T(8,128)(2,1)} %param.13, bf16[1536,256]{1,0:T(8,128)(2,1)} %param.11), kind=kOutput, calls=%fused_computation | convolution fusion | flops 4833411072 | bytes 22806528 | tf_op jit(solution)/shard_map/dot_general | solution.py:28
  28.1 0.0 reduce-scatter.13.cloned.1.call-update
  28.2 0.0 reduce-scatter.23.cloned.1.call-start
  28.2 0.6 copy-done.8
  28.8 0.6 multiply_reduce_fusion.4
  29.4 0.6 multiply_reduce_fusion.5
  30.0 2.5 multiply_convert_fusion
  32.5 28.0 %all_gather.7 = bf16[256,1280]{0,1:T(8,128)(2,1)} all-gather(bf16[256,320]{0,1:T(8,128)(2,1)S(1)} %get-tuple-element.32), channel_id=1, replica_groups=mesh['groups'=2,'tp'=4,'sec'=2,'dp'=2] {'tp'}, dimensions={1}, use_global_device_ids=true | all-gather | bytes 819200 | tf_op jit(solution)/shard_map/all_gather | solution.py:92
  60.6 0.0 copy-done.4
  60.6 1.2 multiply_convert_fusion.1
  61.8 26.9 %all_gather.6 = bf16[256,1280]{0,1:T(8,128)(2,1)} all-gather(bf16[256,320]{0,1:T(8,128)(2,1)S(1)} %get-tuple-element.29), channel_id=1, replica_groups=mesh['groups'=2,'tp'=4,'sec'=2,'dp'=2] {'tp'}, dimensions={1}, use_global_device_ids=true | all-gather | bytes 819200 | tf_op jit(solution)/shard_map/all_gather | solution.py:91
  88.6 4.7 %reduce-scatter.17.cloned.1.call-done = bf16[1280,256]{1,0:T(8,128)(2,1)} async-done(((bf16[5120,256]{1,0:T(8,128)(2,1)}), bf16[1280,256]{1,0:T(8,128)(2,1)}) %reduce-scatter.17.cloned.1.call-update) | async-done | bytes 655376 | tf_op jit(solution)/shard_map/reduce_scatter | solution.py:106
  93.3 0.0 copy-done
  93.3 3.7 multiply_reduce_fusion.2
  97.0 0.6 stack_broadcast_in_dim.7
  97.7 57.9 %reduce-scatter.13.cloned.1.call-done = bf16[1536,256]{1,0:T(8,128)(2,1)} async-done(((bf16[6144,256]{1,0:T(8,128)(2,1)}), bf16[1536,256]{1,0:T(8,128)(2,1)}) %reduce-scatter.13.cloned.1.call-update) | async-done | bytes 786448 | tf_op jit(solution)/shard_map/reduce_scatter | solution.py:100
  155.5 5.3 %multiply_reduce_fusion = (f32[256]{0:T(256)S(1)}, f32[256]{0:T(256)S(1)}, f32[256]{0:T(256)S(1)}, f32[256]{0:T(256)S(1)}, f32[256]{0:T(256)S(1)}, /*index=5*/f3...) fusion(f32[1536]{0:T(1024)S(1)} %copy-done.9, bf16[1536,256]{1,0:T(8,128)(2,1)} %reduce-scatter.13.cloned.1.call-done, ...), kind=kOutput, calls=%fused_computation.38 | convolution fusion | flops 1012529408 | bytes 6960128 | tf_op jit(solution)/shard_map/dot_general | solution.py:94
  160.8 0.6 stack_broadcast_in_dim.6
  161.5 17.5 %all-reduce = (f32[8,256]{1,0:T(8,128)S(1)}, f32[8,256]{1,0:T(8,128)S(1)}) all-reduce(f32[8,256]{1,0:T(8,128)S(1)} %stack.55, f32[8,256]{1,0:T(8,128)S(1)} %stack.63), channel_id=1, replica_groups=mesh['groups'=2,'tp'=4,'sec'=2,'dp'=2] {'tp'}, use_global_device_ids=true, to_apply=%region_9.0 | all-reduce | flops 4096 | bytes 32768 | tf_op jit(solution)/shard_map/psum | solution.py:112
  179.1 1.9 fusion.28
  181.0 0.0 copy-start.3
  181.0 0.8 copy-done.3
  181.9 2.2 fusion.2
  184.1 0.0 reduce-scatter.23.cloned.1.call-update
  184.1 0.0 reduce-scatter.21.cloned.1.call-start
  184.2 2.1 fusion.18
  186.3 0.0 copy-start.2
  186.3 0.9 copy-done.2
  187.2 4.8 %fusion.1 = bf16[1280,256]{1,0:T(8,128)(2,1)} fusion(bf16[1536,256]{1,0:T(8,128)(2,1)S(1)} %fusion.18, bf16[1536,1280]{1,0:T(8,128)(2,1)} %param.20), kind=kOutput, calls=%fused_computation.16 | convolution fusion | flops 1006960640 | bytes 5373952 | tf_op jit(solution)/shard_map/dot_general | solution.py:124
  192.0 0.0 reduce-scatter.21.cloned.1.call-update
  192.0 0.0 reduce-scatter.27.cloned.1.call-start
  192.0 12.8 %reduce-scatter.23.cloned.1.call-done = bf16[320,256]{1,0:T(8,128)(2,1)} async-done(((bf16[1280,256]{1,0:T(8,128)(2,1)}), bf16[320,256]{1,0:T(8,128)(2,1)}) %reduce-scatter.23.cloned.1.call-update) | async-done | bytes 163856 | tf_op jit(solution)/shard_map/reduce_scatter | solution.py:131
  204.8 2.6 convolution_convert_fusion.4
  207.4 2.2 copy.30
  209.7 0.0 reduce-scatter.27.cloned.1.call-update
  209.7 0.0 reduce-scatter.25.cloned.1.call-start
  209.7 18.3 %reduce-scatter.21.cloned.1.call-done = bf16[320,256]{1,0:T(8,128)(2,1)} async-done(((bf16[1280,256]{1,0:T(8,128)(2,1)}), bf16[320,256]{1,0:T(8,128)(2,1)}) %reduce-scatter.21.cloned.1.call-update) | async-done | bytes 163856 | tf_op jit(solution)/shard_map/reduce_scatter | solution.py:123
  228.0 2.6 convolution_convert_fusion.5
  230.7 2.2 copy.28
  232.9 0.0 reduce-scatter.25.cloned.1.call-update
  232.9 0.0 all-reduce.3.cloned.1.call-start
  233.0 0.0 copy-start.5
  233.0 2.0 fusion.65
  235.1 1.5 fusion
  236.5 0.0 all-reduce.3.cloned.1.call-update
  236.5 0.0 reduce-scatter.19.cloned.1.call-start
  236.6 4.1 convolution_convert_fusion.1
  240.7 0.0 reduce-scatter.19.cloned.1.call-update
  240.7 0.0 reduce-scatter.15.cloned.1.call-start
  240.8 4.4 %convolution_convert_fusion.2 = bf16[1536,1280]{0,1:T(8,128)(2,1)} fusion(bf16[1536,256]{1,0:T(8,128)(2,1)} %copy-done.2, bf16[256,1280]{0,1:T(8,128)(2,1)} %all_gather.6), kind=kOutput, calls=%fused_computation.2 | convolution fusion | flops 1008599040 | bytes 5373952 | tf_op jit(solution)/shard_map/dot_general | solution.py:121
  245.2 0.0 reduce-scatter.15.cloned.1.call-update
  245.2 8.6 %reduce-scatter.27.cloned.1.call-done = bf16[320,320]{1,0:T(8,128)(2,1)} async-done(((bf16[1280,320]{1,0:T(8,128)(2,1)}), bf16[320,320]{1,0:T(8,128)(2,1)}) %reduce-scatter.27.cloned.1.call-update) | async-done | bytes 204816
  253.9 1.8 copy.31
  255.7 25.3 %reduce-scatter.25.cloned.1.call-done = bf16[320,320]{1,0:T(8,128)(2,1)} async-done(((bf16[1280,320]{1,0:T(8,128)(2,1)}), bf16[320,320]{1,0:T(8,128)(2,1)}) %reduce-scatter.25.cloned.1.call-update) | async-done | bytes 204816
  281.0 1.8 copy.29
  282.8 41.1 %all-reduce.3.cloned.1.call-done = bf16[256,1280]{1,0:T(8,128)(2,1)} async-done(((bf16[256,1280]{1,0:T(8,128)(2,1)}), bf16[256,1280]{1,0:T(8,128)(2,1)}) %all-reduce.3.cloned.1.call-update) | async-done | bytes 655376 | tf_op jit(solution)/shard_map/psum | solution.py:149
  323.9 41.4 %reduce-scatter.19.cloned.1.call-done = bf16[1280,320]{0,1:T(8,128)(2,1)} async-done(((bf16[1280,1280]{0,1:T(8,128)(2,1)}), bf16[1280,320]{0,1:T(8,128)(2,1)}) %reduce-scatter.19.cloned.1.call-update) | async-done | bytes 819216 | tf_op jit(solution)/shard_map/reduce_scatter | solution.py:154
  365.3 46.2 %reduce-scatter.15.cloned.1.call-done = bf16[1536,320]{0,1:T(8,128)(2,1)} async-done(((bf16[1536,1280]{0,1:T(8,128)(2,1)}), bf16[1536,320]{0,1:T(8,128)(2,1)}) %reduce-scatter.15.cloned.1.call-update) | async-done | bytes 983056 | tf_op jit(solution)/shard_map/reduce_scatter | solution.py:151
  411.5 2.0 copy.33
  (16 shorter events, 0.1 us)
Async XLA Ops:
  7.2 86.1 %copy-start = (bf16[1280,1280]{1,0:T(8,128)(2,1)S(1)}, bf16[1280,1280]{1,0:T(8,128)(2,1)}, u32[]{:S(2)}) copy-start(bf16[1280,1280]{1,0:T(8,128)(2,1)} %param.21) | copy-start | bytes 9830404
  7.2 86.1 %reduce-scatter.17.cloned.1.call-start = ((), (), s32[]{:S(2)}) async-start(), calls=%async_computation.10 | async-start | bytes 3276800 | tf_op jit(solution)/shard_map/reduce_scatter | solution.py:106
  17.5 138.0 %reduce-scatter.13.cloned.1.call-start = ((), (), s32[]{:S(2)}) async-start(), calls=%async_computation.8 | async-start | bytes 3932160 | tf_op jit(solution)/shard_map/reduce_scatter | solution.py:100
  28.1 0.7 copy-start.8
  28.1 1.3 copy-start.9
  28.2 176.7 %reduce-scatter.23.cloned.1.call-start = ((), (), s32[]{:S(2)}) async-start(), calls=%async_computation.13 | async-start | bytes 819200 | tf_op jit(solution)/shard_map/reduce_scatter | solution.py:131
  28.8 31.8 %copy-start.1 = (bf16[256,1280]{1,0:T(8,128)(2,1)S(1)}, bf16[256,1280]{1,0:T(8,128)(2,1)}, u32[]{:S(2)}) copy-start(bf16[256,1280]{1,0:T(8,128)(2,1)} %param.17) | copy-start | bytes 1966084
  28.8 31.8 %copy-start.4 = (bf16[320,1280]{1,0:T(8,128)(2,1)S(1)}, bf16[320,1280]{1,0:T(8,128)(2,1)}, u32[]{:S(2)}) copy-start(bf16[320,1280]{1,0:T(8,128)(2,1)} %param.18) | copy-start | bytes 2457604
  181.0 0.8 copy-start.3
  184.1 43.9 %reduce-scatter.21.cloned.1.call-start = ((), (), s32[]{:S(2)}) async-start(), calls=%async_computation.12 | async-start | bytes 819200 | tf_op jit(solution)/shard_map/reduce_scatter | solution.py:123
  186.3 0.9 copy-start.2
  192.0 61.9 %reduce-scatter.27.cloned.1.call-start = ((), (), s32[]{:S(2)}) async-start(), calls=%async_computation.16 | async-start | bytes 1228800
  209.7 71.3 %reduce-scatter.25.cloned.1.call-start = ((), (), s32[]{:S(2)}) async-start(), calls=%async_computation.15 | async-start | bytes 1228800
  232.9 2.1 copy-start.7
  232.9 91.0 %all-reduce.3.cloned.1.call-start = ((), (), s32[]{:S(2)}) async-start(), calls=%async_computation.14 | async-start | bytes 1310720 | tf_op jit(solution)/shard_map/psum | solution.py:149
  233.0 2.1 copy-start.5
  233.0 2.1 copy-start.6
  236.5 128.8 %reduce-scatter.19.cloned.1.call-start = ((), (), s32[]{:S(2)}) async-start(), calls=%async_computation.11 | async-start | bytes 4096000 | tf_op jit(solution)/shard_map/reduce_scatter | solution.py:154
  240.7 170.8 %reduce-scatter.15.cloned.1.call-start = ((), (), s32[]{:S(2)}) async-start(), calls=%async_computation.9 | async-start | bytes 4915200 | tf_op jit(solution)/shard_map/reduce_scatter | solution.py:151
Sparse Core Ops, SparseCore 0:
  17.6 75.6 reduce-scatter.16
  95.6 59.9 reduce-scatter.12
  184.2 20.5 reduce-scatter.22
  207.0 21.0 reduce-scatter.20
  230.5 23.3 reduce-scatter.26
  256.5 24.4 reduce-scatter.24
  283.4 40.4 all-reduce.2
  327.0 38.2 reduce-scatter.18
  368.6 42.8 reduce-scatter.14

commit v2 on v1

v2 whole, which is shorter than its diff:
```python
import math

import jax
import jax.numpy as jnp
from jax import lax
from jax.sharding import PartitionSpec as P

EPSILON = 1e-06
CONTRACT_FIRST = (((0,), (0,)), ((), ()))
CONTRACT_LAST = (((1,), (1,)), ((), ()))


def normal_cdf(values):
    return 0.5 * (1.0 + lax.erf(values * (1.0 / math.sqrt(2.0))))


def gelu_value(values):
    return values * normal_cdf(values)


def gelu_slope(values):
    return normal_cdf(values) + values * jnp.exp(-0.5 * values * values) * (
        1.0 / math.sqrt(2.0 * math.pi)
    )


def project_teacher(weight_rows, context):
    return lax.dot_general(weight_rows, context, CONTRACT_FIRST, preferred_element_type=jnp.float32)


def token_sums(own, gain_rows, predicted):
    gain = gain_rows[:, None]
    scaled = gain * own
    return jnp.stack(
        (
            jnp.sum(own, axis=0),
            jnp.sum(own * own, axis=0),
            jnp.sum(predicted * predicted, axis=0),
            jnp.sum(scaled * predicted, axis=0),
            jnp.sum(gain * predicted, axis=0),
            jnp.sum(scaled * scaled, axis=0),
            jnp.sum(gain * scaled, axis=0),
            jnp.broadcast_to(jnp.sum(gain * gain), own.shape[1:]),
        )
    )


def make_slope(own, gain_rows, predicted, sums, width):
    average = sums[0] / width
    inverse = lax.rsqrt(sums[1] / width - average * average + EPSILON)
    pred_sq = sums[2]
    inner = inverse * (sums[3] - average * sums[4])
    target_sq = inverse * inverse * (
        sums[5] - 2.0 * average * sums[6] + average * average * sums[7]
    )
    inv_pred = lax.rsqrt(pred_sq + EPSILON)
    inv_target = lax.rsqrt(target_sq + EPSILON)
    cosine = inner * inv_pred * inv_target
    weight = width / 8.0
    target = gain_rows[:, None] * (own - average) * inverse
    slope = -weight * (
        target * (inv_pred * inv_target) - predicted * (cosine * inv_pred * inv_pred)
    )
    return slope.astype(jnp.bfloat16)


def tp_shift(value, step):
    count = lax.axis_size("tp")
    return lax.ppermute(value, "tp", [(i, (i + step) % count) for i in range(count)])


def tp_sum(value):
    count = lax.axis_size("tp")
    parts = [tp_shift(value, step) for step in range(1, count)]
    own = lax.axis_index("tp")
    stacked = jnp.zeros((count,) + value.shape, value.dtype)
    stacked = lax.dynamic_update_index_in_dim(stacked, value, own, 0)
    for step, part in enumerate(parts, 1):
        stacked = lax.dynamic_update_index_in_dim(stacked, part, (own - step) % count, 0)
    return jnp.sum(stacked, axis=0)


def tp_columns(value):
    count = lax.axis_size("tp")
    share = value.shape[1]
    own = lax.axis_index("tp")
    parts = [value] + [tp_shift(value, step) for step in range(1, count)]
    full = jnp.zeros((value.shape[0], share * count), value.dtype)
    for step, part in enumerate(parts):
        full = lax.dynamic_update_slice_in_dim(full, part, ((own - step) % count) * share, 1)
    return full


def summed_product(left, right):
    sections, cores = lax.axis_size("sec"), lax.axis_size("dp")
    if sections != 2 or cores != 2:
        product = jnp.dot(left, right, preferred_element_type=jnp.float32)
        return lax.psum_scatter(
            product.astype(jnp.bfloat16), ("sec", "dp"), scatter_dimension=1, tiled=True
        )
    share = right.shape[1] // 4
    sec, core = lax.axis_index("sec"), lax.axis_index("dp")
    swap = [(0, 1), (1, 0)]

    def piece(section, which):
        columns = lax.dynamic_slice_in_dim(right, (section * 2 + which) * share, share, 1)
        return jnp.dot(left, columns, preferred_element_type=jnp.float32)

    far = lax.ppermute(piece(1 - sec, 1 - core).astype(jnp.bfloat16), "dp", swap)
    near = lax.ppermute(piece(sec, 1 - core).astype(jnp.bfloat16), "dp", swap)
    other = lax.ppermute(
        (piece(1 - sec, core) + far.astype(jnp.float32)).astype(jnp.bfloat16), "sec", swap
    )
    total = piece(sec, core) + near.astype(jnp.float32) + other.astype(jnp.float32)
    return total.astype(jnp.bfloat16)


def own_rows(weight_rows, context):
    return lax.psum_scatter(
        project_teacher(weight_rows, context).astype(jnp.bfloat16),
        "tp",
        scatter_dimension=0,
        tiled=True,
    ).astype(jnp.float32)


def local(
    giant_context,
    clip_context,
    giant_out,
    clip_out,
    giant_gain,
    clip_gain,
    student_features,
    giant_first,
    clip_first,
    giant_head,
    clip_head,
):
    giant_width = giant_out.shape[1]
    clip_width = clip_out.shape[1]
    clip_own = own_rows(clip_out, clip_context)
    giant_own = own_rows(giant_out, giant_context)
    clip_pre = lax.dot_general(
        student_features, clip_first, CONTRACT_LAST, preferred_element_type=jnp.float32
    )
    giant_pre = lax.dot_general(
        student_features, giant_first, CONTRACT_LAST, preferred_element_type=jnp.float32
    )
    clip_hidden = tp_columns(gelu_value(clip_pre).astype(jnp.bfloat16))
    giant_hidden = tp_columns(gelu_value(giant_pre).astype(jnp.bfloat16))
    clip_pred = lax.dot_general(
        clip_head, clip_hidden, CONTRACT_LAST, preferred_element_type=jnp.float32
    )
    giant_pred = lax.dot_general(
        giant_head, giant_hidden, CONTRACT_LAST, preferred_element_type=jnp.float32
    )
    clip_stats = tp_sum(token_sums(clip_own, clip_gain, clip_pred))
    clip_slope = make_slope(clip_own, clip_gain, clip_pred, clip_stats, clip_width)
    clip_grad = summed_product(clip_slope, clip_hidden)
    clip_back = lax.dot_general(
        clip_head, clip_slope, CONTRACT_FIRST, preferred_element_type=jnp.float32
    ).astype(jnp.bfloat16)
    giant_stats = tp_sum(token_sums(giant_own, giant_gain, giant_pred))
    giant_slope = make_slope(giant_own, giant_gain, giant_pred, giant_stats, giant_width)
    giant_back = lax.dot_general(
        giant_head, giant_slope, CONTRACT_FIRST, preferred_element_type=jnp.float32
    ).astype(jnp.bfloat16)
    back = lax.psum_scatter(
        jnp.concatenate((giant_back, clip_back), axis=1), "tp", scatter_dimension=0, tiled=True
    ).astype(jnp.float32)
    giant_grad = summed_product(giant_slope, giant_hidden)
    tokens = student_features.shape[0]
    giant_pslope = (back[:, :tokens] * gelu_slope(giant_pre.T)).astype(jnp.bfloat16)
    clip_pslope = (back[:, tokens:] * gelu_slope(clip_pre.T)).astype(jnp.bfloat16)
    feature_term = lax.dot_general(
        giant_pslope, giant_first, CONTRACT_FIRST, preferred_element_type=jnp.float32
    )
    feature_term = feature_term + lax.dot_general(
        clip_pslope, clip_first, CONTRACT_FIRST, preferred_element_type=jnp.float32
    )
    feature_sum = lax.psum(feature_term.astype(jnp.bfloat16), "tp")
    giant_first_grad = summed_product(giant_pslope, student_features)
    clip_first_grad = summed_product(clip_pslope, student_features)
    return (giant_grad, clip_grad, giant_first_grad, clip_first_grad, feature_sum)


def solution(mesh):
    placed = (
        P("tp", ("groups", "sec", "dp")),
        P("tp", ("groups", "sec", "dp")),
        P("tp", None),
        P("tp", None),
        P("tp"),
        P("tp"),
        P(("groups", "sec", "dp"), None),
        P("tp", None),
        P("tp", None),
        P("tp", None),
        P("tp", None),
    )
    return jax.shard_map(
        local,
        mesh=mesh,
        in_specs=placed,
        out_specs=(
            P(("groups", "tp"), ("sec", "dp")),
            P(("groups", "tp"), ("sec", "dp")),
            P(("groups", "tp"), ("sec", "dp")),
            P(("groups", "tp"), ("sec", "dp")),
            P(("groups", "sec", "dp"), None),
        ),
        check_vma=False,
    )
```

time: 421 us -> 305 us (0.72)
  waiting for transfers between devices: 256 us -> 159 us
  blocking collectives: 72.4 us -> 0 us
  starting transfers between devices: 0.37 us -> 35.8 us
  matrix products: 57.8 us -> 72 us
  other arithmetic: 5.31 us -> 10.6 us
    reduce_scatter x6 -> x3, waiting for transfers between devices: 181 us -> 53.9 us  [the longest x2 53.9 us: own_rows(): lax.psum_scatter(project_teacher(weight_rows, context).astype(jnp.bfloat1...]
    ppermute x0 -> x24, waiting for transfers between devices: none -> 80.4 us  [the longest x4 42.8 us: summed_product(): lax.ppermute((piece(1 - sec, core) + far.astype(jnp.float32)).astype(jnp....]
    all_gather x2 -> x0, blocking collectives: 54.9 us -> none  [the longest x1 28 us: local(): lax.all_gather(clip_hidden_own, 'tp', axis=1, tiled=True)]
    ppermute x0 -> x24, starting transfers between devices: none -> 35.6 us  [the longest x12 29.4 us: tp_shift(): lax.ppermute(value, 'tp', [(i, (i + step) % count) for i in range(count)])]
    unnamed x11 -> x4, waiting for transfers between devices: 34.1 us -> 0.07 us
    psum x1 -> x0, blocking collectives: 17.5 us -> none  [local(): lax.psum((token_sums(giant_own, giant_gain, giant_pred), token_sums(clip_...]
    psum x1, waiting for transfers between devices: 41.1 us -> 24.6 us  [local(): feature_sum = lax.psum(feature_term.astype(jnp.bfloat16), 'tp')]
    dot_general x4 -> x16, matrix products: 13.8 us -> 30.2 us  [piece(): return jnp.dot(left, columns, preferred_element_type=jnp.float32)]
  transfers between devices with their start and end apart: 9 -> 28, of which waited for: 9 -> 15; matrix products, arithmetic and copies ran while one was open for 12% -> 20% of each run, Pallas kernels for 0% -> 0%
where the time goes in v2:
time: 305 us
  waiting for transfers between devices  159 us (52%)
  matrix products  72 us (24%)
  starting transfers between devices  35.8 us (12%)
  between operations  14.1 us (5%)
  local copies, waits for them, and re-layouts  13.1 us (4%)
  other arithmetic  10.6 us (3%)
    reduce_scatter x2, waiting for transfers between devices, own_rows(): lax.psum_scatter(project_teacher(weight_rows, context).astype(jnp.bfloat1...  53.9 us
    ppermute x4, waiting for transfers between devices, summed_product(): lax.ppermute((piece(1 - sec, core) + far.astype(jnp.float32)).astype(jnp....  42.8 us
    ppermute x12, waiting for transfers between devices, tp_shift(): lax.ppermute(value, 'tp', [(i, (i + step) % count) for i in range(count)])  37.6 us
    dot_general x16, matrix products, piece(): return jnp.dot(left, columns, preferred_element_type=jnp.float32)  30.2 us
    ppermute x12, starting transfers between devices, tp_shift(): lax.ppermute(value, 'tp', [(i, (i + step) % count) for i in range(count)])  29.4 us
    psum x1, waiting for transfers between devices, local(): feature_sum = lax.psum(feature_term.astype(jnp.bfloat16), 'tp')  24.6 us
    dot_general x2, matrix products, project_teacher(): lax.dot_general(weight_rows, context, CONTRACT_FIRST, preferred_element_t...  20.8 us
    dynamic_update_slice x6, local copies, waits for them, and re-layouts, tp_columns(): lax.dynamic_update_slice_in_dim(full, part, (own - step) % count * share, 1)  8.67 us
  transfers between devices with their start and end apart: 28, of which 15 were waited for; matrix products, arithmetic and copies ran while one was open for 20% of the time, Pallas kernels for 0%

profile of v2, /device:TPU:0, one launch (start us, length us, event | category | flops | bytes accessed | tf_op | source)
XLA Modules:
  0.0 304.6 jit_solution(10511319935148046687)
XLA Ops:
  7.2 10.2 %convolution_convert_fusion.1 = bf16[5120,256]{1,0:T(8,128)(2,1)} fusion(bf16[1280,5120]{1,0:T(8,128)(2,1)} %param.14, bf16[1280,256]{1,0:T(8,128)(2,1)} %param.12), kind=kOutput, calls=%fused_computation.1 | convolution fusion | flops 3356753920 | bytes 16384000 | tf_op jit(solution)/shard_map/dot_general | solution.py:28
  17.5 10.6 %convolution_convert_fusion = bf16[6144,256]{1,0:T(8,128)(2,1)} fusion(bf16[1536,6144]{1,0:T(8,128)(2,1)} %param.13, bf16[1536,256]{1,0:T(8,128)(2,1)} %param.11), kind=kOutput, calls=%fused_computation | convolution fusion | flops 4833411072 | bytes 22806528 | tf_op jit(solution)/shard_map/dot_general | solution.py:28
  28.3 2.6 constant_dynamic-update-slice_fusion.7
  30.9 3.0 collective-permute-start
  34.0 2.6 collective-permute-start.1
  36.5 1.4 collective-permute-start.2
  38.0 1.2 constant_dynamic-update-slice_fusion.3
  39.2 0.9 copy-done.14
  42.3 2.3 collective-permute-done
  44.6 4.9 %collective-permute-start.11 = (bf16[256,320]{0,1:T(8,128)(2,1)}, bf16[256,320]{0,1:T(8,128)(2,1)S(1)}, u32[]{:S(2)}, u32[]{:S(2)}) collective-permute-start(bf16[256,320]{0,1:T(8,128)(2,1)} %get-tuple-element.23), channel_id=1, source_target_pairs={{0,12},{4,0},{8,4},{12,8},{1,13},{5,1},{9,5},{13,9},{2,14},{6,2},{... | collective-permute-start | bytes 491528 | tf_op jit(solution)/shard_map/ppermute | solution.py:69
  49.5 1.6 constant_dynamic-update-slice_fusion.6
  51.1 14.5 %collective-permute-done.9 = bf16[256,320]{0,1:T(8,128)(2,1)} collective-permute-done((bf16[256,320]{0,1:T(8,128)(2,1)}, bf16[256,320]{0,1:T(8,128)(2,1)}, u32[]{:S(2)}, u32[]{:S(2)}) %collective-permute-start.9) | collective-permute-done | bytes 163872 | tf_op jit(solution)/shard_map/ppermute | solution.py:69
  65.7 1.6 constant_dynamic-update-slice_fusion.2
  67.3 1.6 constant_dynamic-update-slice_fusion.5
  68.9 17.7 %collective-permute-done.10 = bf16[256,320]{0,1:T(8,128)(2,1)} collective-permute-done((bf16[256,320]{0,1:T(8,128)(2,1)}, bf16[256,320]{0,1:T(8,128)(2,1)}, u32[]{:S(2)}, u32[]{:S(2)}) %collective-permute-start.10) | collective-permute-done | bytes 163872 | tf_op jit(solution)/shard_map/ppermute | solution.py:69
  86.6 1.6 constant_dynamic-update-slice_fusion.1
  88.1 1.6 constant_dynamic-update-slice_fusion.4
  89.7 0.7 constant_dynamic-update-slice_fusion
  90.5 2.8 reduce-scatter.6.cloned.1.call-done
  93.3 3.7 %multiply_reduce_fusion.2 = (f32[256]{0:T(256)S(1)}, f32[256]{0:T(256)S(1)}, f32[256]{0:T(256)S(1)}, f32[256]{0:T(256)S(1)}, f32[256]{0:T(256)S(1)}, /*index=5*/...) fusion(f32[1280]{0:T(1024)S(1)} %copy-done.17, bf16[1280,256]{1,0:T(8,128)(2,1)} %reduce-scatter.6.cloned.1.call-done, ...), kind=kOutput, calls=%fused_computation.61 | convolution fusion | flops 843774208 | bytes 5910528 | tf_op jit(solution)/shard_map/dot_general | solution.py:152
  97.7 8.0 %collective-permute-start.12 = (f32[8,256]{1,0:T(8,128)S(1)}, f32[8,256]{1,0:T(8,128)S(1)}, u32[]{:S(2)}, u32[]{:S(2)}) collective-permute-start(f32[8,256]{1,0:T(8,128)S(1)} %stack.63), channel_id=1, source_target_pairs={{0,4},{4,8},{8,12},{12,0},{1,5},{5,9},{9,13},{13,1},{2,6},{6,10},{... | collective-permute-start | bytes 24584 | tf_op jit(solution)/shard_map/ppermute | solution.py:69
  105.6 2.1 collective-permute-start.13
  107.7 0.8 collective-permute-start.14
  108.9 1.4 collective-permute-done.13
  110.3 51.1 %reduce-scatter.4.cloned.1.call-done = bf16[1536,256]{1,0:T(8,128)(2,1)} async-done(((bf16[6144,256]{1,0:T(8,128)(2,1)}), bf16[1536,256]{1,0:T(8,128)(2,1)}) %reduce-scatter.4.cloned.1.call-update) | async-done | bytes 786448 | tf_op jit(solution)/shard_map/reduce_scatter | solution.py:119
  161.4 5.3 %multiply_reduce_fusion = (f32[256]{0:T(256)S(1)}, f32[256]{0:T(256)S(1)}, f32[256]{0:T(256)S(1)}, f32[256]{0:T(256)S(1)}, f32[256]{0:T(256)S(1)}, /*index=5*/f3...) fusion(f32[1536]{0:T(1024)S(1)} %copy-done.18, bf16[1536,256]{1,0:T(8,128)(2,1)} %reduce-scatter.4.cloned.1.call-done, ...), kind=kOutput, calls=%fused_computation.48 | convolution fusion | flops 1012529408 | bytes 6960128 | tf_op jit(solution)/shard_map/dot_general | solution.py:155
  167.4 1.4 collective-permute-start.3
  168.8 1.6 collective-permute-start.4
  170.4 2.6 collective-permute-start.5
  173.4 0.9 collective-permute-done.5
  174.4 1.9 fusion.34
  176.3 2.2 fusion.8
  178.6 2.1 fusion.24
  180.8 4.1 %fusion.7 = bf16[1280,256]{1,0:T(8,128)(2,1)S(1)} fusion(bf16[1536,256]{1,0:T(8,128)(2,1)S(1)} %fusion.24, bf16[1536,1280]{1,0:T(8,128)(2,1)} %param.20), kind=kOutput, calls=%fused_computation.26 | convolution fusion | flops 1006960640 | bytes 5373952 | tf_op jit(solution)/shard_map/dot_general | solution.py:166
  184.9 1.2 pad_maximum_fusion
  186.1 2.5 convolution_convert_fusion.4
  188.6 2.3 convolution_convert_fusion.2
  191.4 2.5 convolution_convert_fusion.5
  194.0 2.3 convolution_convert_fusion.3
  196.8 2.5 fusion.4
  199.4 1.5 collective-permute-start.17
  200.8 2.7 fusion.5
  204.1 16.7 %collective-permute-done.17 = bf16[1280,320]{0,1:T(8,128)(2,1)} collective-permute-done((bf16[1280,320]{0,1:T(8,128)(2,1)}, bf16[1280,320]{0,1:T(8,128)(2,1)}, u32[]{:S(2)}, u32[]{:S(2)}) %collective-permute-start.17) | collective-permute-done | bytes 819232 | tf_op jit(solution)/shard_map/ppermute | solution.py:111
  220.8 3.0 fusion.3
  223.8 17.1 %collective-permute-done.8 = bf16[1536,320]{0,1:T(8,128)(2,1)} collective-permute-done((bf16[1536,320]{0,1:T(8,128)(2,1)}, bf16[1536,320]{0,1:T(8,128)(2,1)}, u32[]{:S(2)}, u32[]{:S(2)}) %collective-permute-start.8) | collective-permute-done | bytes 983072 | tf_op jit(solution)/shard_map/ppermute | solution.py:111
  240.9 3.0 fusion.2
  243.9 1.1 convert_element_type.158
  245.1 1.4 fusion.46
  246.5 1.1 convolution_convert_fusion.8
  247.6 1.0 convolution_convert_fusion.9
  248.6 1.1 fusion.65
  250.2 1.0 convolution_convert_fusion.10
  251.3 1.0 convolution_convert_fusion.11
  252.3 1.4 fusion.6
  254.8 1.3 fusion.67
  256.1 1.4 add_convert_fusion.1
  257.5 1.5 collective-permute-start.23
  259.0 1.3 add_convert_fusion.3
  260.9 5.4 %collective-permute-done.23 = bf16[320,320]{1,0:T(8,128)(2,1)S(1)} collective-permute-done((bf16[320,320]{1,0:T(8,128)(2,1)S(1)}, bf16[320,320]{1,0:T(8,128)(2,1)S(1)}, u32[]{:S(2)}, u32[]{:S(2)}) %collective-permute-start.23) | collective-permute-done | bytes 204832 | tf_op jit(solution)/shard_map/ppermute | solution.py:111
  266.4 0.8 add_convert_fusion
  267.1 3.6 %collective-permute-done.20 = bf16[320,320]{1,0:T(8,128)(2,1)S(1)} collective-permute-done((bf16[320,320]{1,0:T(8,128)(2,1)S(1)}, bf16[320,320]{1,0:T(8,128)(2,1)S(1)}, u32[]{:S(2)}, u32[]{:S(2)}) %collective-permute-start.20) | collective-permute-done | bytes 204832 | tf_op jit(solution)/shard_map/ppermute | solution.py:111
  270.7 0.8 add_convert_fusion.2
  271.5 24.6 %all-reduce.2.cloned.1.call-done = bf16[256,1280]{1,0:T(8,128)(2,1)} async-done(((bf16[256,1280]{1,0:T(8,128)(2,1)}), bf16[256,1280]{1,0:T(8,128)(2,1)}) %all-reduce.2.cloned.1.call-update) | async-done | bytes 655376 | tf_op jit(solution)/shard_map/psum | solution.py:182
  296.1 2.0 copy.47
  (97 shorter events, 8.7 us)
Async XLA Ops:
  7.2 86.1 %copy-start = (bf16[1280,1280]{1,0:T(8,128)(2,1)S(1)}, bf16[1280,1280]{1,0:T(8,128)(2,1)}, u32[]{:S(2)}) copy-start(bf16[1280,1280]{1,0:T(8,128)(2,1)} %param.21) | copy-start | bytes 9830404
  7.2 86.1 %reduce-scatter.6.cloned.1.call-start = ((), (), s32[]{:S(2)}) async-start(), calls=%async_computation.4 | async-start | bytes 3276800 | tf_op jit(solution)/shard_map/reduce_scatter | solution.py:119
  17.5 143.9 %reduce-scatter.4.cloned.1.call-start = ((), (), s32[]{:S(2)}) async-start(), calls=%async_computation.3 | async-start | bytes 3932160 | tf_op jit(solution)/shard_map/reduce_scatter | solution.py:119
  28.1 215.8 %reduce-scatter.8.cloned.1.call-start = ((), (), s32[]{:S(2)}) async-start(), calls=%async_computation.5 | async-start | bytes 1638400 | tf_op jit(solution)/shard_map/reduce_scatter | solution.py:169
  28.2 9.7 %copy-start.7 = (bf16[256,1280]{1,0:T(8,128)(2,1)S(1)}, bf16[256,1280]{1,0:T(8,128)(2,1)}, u32[]{:S(2)}) copy-start(bf16[256,1280]{1,0:T(8,128)(2,1)} %param.17) | copy-start | bytes 1966084
  28.2 9.7 %copy-start.11 = (bf16[320,1280]{1,0:T(8,128)(2,1)S(1)}, bf16[320,1280]{1,0:T(8,128)(2,1)}, u32[]{:S(2)}) copy-start(bf16[320,1280]{1,0:T(8,128)(2,1)} %param.19) | copy-start | bytes 2457604
  30.9 8.3 %copy-start.13 = (bf16[256,1280]{0,1:T(8,128)(2,1)}, bf16[256,1280]{0,1:T(8,128)(2,1)S(1)}, u32[]{:S(2)}) copy-start(bf16[256,1280]{0,1:T(8,128)(2,1)S(1)} %get-tuple-element.27) | copy-start | bytes 1966084
  30.9 10.2 %copy-start.18 = (f32[1536]{0:T(1024)S(1)}, f32[1536]{0:T(1024)}, u32[]{:S(2)}) copy-start(f32[1536]{0:T(1024)} %param.15) | copy-start | bytes 18436
  30.9 10.8 %copy-start.17 = (f32[1280]{0:T(1024)S(1)}, f32[1280]{0:T(1024)}, u32[]{:S(2)}) copy-start(f32[1280]{0:T(1024)} %param.16) | copy-start | bytes 15364
  30.9 13.7 %collective-permute-start = (bf16[256,320]{0,1:T(8,128)(2,1)S(1)}, bf16[256,320]{0,1:T(8,128)(2,1)}, u32[]{:S(2)}, u32[]{:S(2)}) collective-permute-start(bf16[256,320]{0,1:T(8,128)(2,1)S(1)} %get-tuple-element.28), channel_id=1, source_target_pairs={{0,4},{4,8},{8,12},{12,0},{1,5},{5,9},{9,13},{13,1},{2,6},{6,10},{... | collective-permute-start | bytes 491528 | tf_op jit(solution)/shard_map/ppermute | solution.py:69
  34.0 33.3 %collective-permute-start.1 = (bf16[256,320]{0,1:T(8,128)(2,1)S(1)}, bf16[256,320]{0,1:T(8,128)(2,1)}, u32[]{:S(2)}, u32[]{:S(2)}) collective-permute-start(bf16[256,320]{0,1:T(8,128)(2,1)S(1)} %get-tuple-element.28), channel_id=1, source_target_pairs={{0,8},{4,12},{8,0},{12,4},{1,9},{5,13},{9,1},{13,5},{2,10},{6,14},... | collective-permute-start | bytes 491528 | tf_op jit(solution)/shard_map/ppermute | solution.py:69
  36.5 51.6 %collective-permute-start.2 = (bf16[256,320]{0,1:T(8,128)(2,1)S(1)}, bf16[256,320]{0,1:T(8,128)(2,1)}, u32[]{:S(2)}, u32[]{:S(2)}) collective-permute-start(bf16[256,320]{0,1:T(8,128)(2,1)S(1)} %get-tuple-element.28), channel_id=1, source_target_pairs={{0,12},{4,0},{8,4},{12,8},{1,13},{5,1},{9,5},{13,9},{2,14},{6,2},{... | collective-permute-start | bytes 491528 | tf_op jit(solution)/shard_map/ppermute | solution.py:69
  39.2 0.9 copy-start.14
  40.1 25.6 %collective-permute-start.9 = (bf16[256,320]{0,1:T(8,128)(2,1)}, bf16[256,320]{0,1:T(8,128)(2,1)}, u32[]{:S(2)}, u32[]{:S(2)}) collective-permute-start(bf16[256,320]{0,1:T(8,128)(2,1)} %get-tuple-element.23), channel_id=1, source_target_pairs={{0,4},{4,8},{8,12},{12,0},{1,5},{5,9},{9,13},{13,1},{2,6},{6,10},{... | collective-permute-start | bytes 491528 | tf_op jit(solution)/shard_map/ppermute | solution.py:69
  40.8 45.8 %collective-permute-start.10 = (bf16[256,320]{0,1:T(8,128)(2,1)}, bf16[256,320]{0,1:T(8,128)(2,1)}, u32[]{:S(2)}, u32[]{:S(2)}) collective-permute-start(bf16[256,320]{0,1:T(8,128)(2,1)} %get-tuple-element.23), channel_id=1, source_target_pairs={{0,8},{4,12},{8,0},{12,4},{1,9},{5,13},{9,1},{13,5},{2,10},{6,14},... | collective-permute-start | bytes 491528 | tf_op jit(solution)/shard_map/ppermute | solution.py:69
  44.6 45.1 %collective-permute-start.11 = (bf16[256,320]{0,1:T(8,128)(2,1)}, bf16[256,320]{0,1:T(8,128)(2,1)S(1)}, u32[]{:S(2)}, u32[]{:S(2)}) collective-permute-start(bf16[256,320]{0,1:T(8,128)(2,1)} %get-tuple-element.23), channel_id=1, source_target_pairs={{0,12},{4,0},{8,4},{12,8},{1,13},{5,1},{9,5},{13,9},{2,14},{6,2},{... | collective-permute-start | bytes 491528 | tf_op jit(solution)/shard_map/ppermute | solution.py:69
  97.7 11.2 %collective-permute-start.12 = (f32[8,256]{1,0:T(8,128)S(1)}, f32[8,256]{1,0:T(8,128)S(1)}, u32[]{:S(2)}, u32[]{:S(2)}) collective-permute-start(f32[8,256]{1,0:T(8,128)S(1)} %stack.63), channel_id=1, source_target_pairs={{0,4},{4,8},{8,12},{12,0},{1,5},{5,9},{9,13},{13,1},{2,6},{6,10},{... | collective-permute-start | bytes 24584 | tf_op jit(solution)/shard_map/ppermute | solution.py:69
  105.6 4.7 %collective-permute-start.13 = (f32[8,256]{1,0:T(8,128)S(1)}, f32[8,256]{1,0:T(8,128)S(1)}, u32[]{:S(2)}, u32[]{:S(2)}) collective-permute-start(f32[8,256]{1,0:T(8,128)S(1)} %stack.63), channel_id=1, source_target_pairs={{0,8},{4,12},{8,0},{12,4},{1,9},{5,13},{9,1},{13,5},{2,10},{6,14},... | collective-permute-start | bytes 24584 | tf_op jit(solution)/shard_map/ppermute | solution.py:69
  107.7 65.7 %collective-permute-start.14 = (f32[8,256]{1,0:T(8,128)S(1)}, f32[8,256]{1,0:T(8,128)S(1)}, u32[]{:S(2)}, u32[]{:S(2)}) collective-permute-start(f32[8,256]{1,0:T(8,128)S(1)} %stack.63), channel_id=1, source_target_pairs={{0,12},{4,0},{8,4},{12,8},{1,13},{5,1},{9,5},{13,9},{2,14},{6,2},{... | collective-permute-start | bytes 24584 | tf_op jit(solution)/shard_map/ppermute | solution.py:69
  167.4 5.7 %collective-permute-start.3 = (f32[8,256]{1,0:T(8,128)S(1)}, f32[8,256]{1,0:T(8,128)S(1)}, u32[]{:S(2)}, u32[]{:S(2)}) collective-permute-start(f32[8,256]{1,0:T(8,128)S(1)} %stack.55), channel_id=1, source_target_pairs={{0,4},{4,8},{8,12},{12,0},{1,5},{5,9},{9,13},{13,1},{2,6},{6,10},{... | collective-permute-start | bytes 24584 | tf_op jit(solution)/shard_map/ppermute | solution.py:69
  168.8 4.6 %collective-permute-start.4 = (f32[8,256]{1,0:T(8,128)S(1)}, f32[8,256]{1,0:T(8,128)S(1)}, u32[]{:S(2)}, u32[]{:S(2)}) collective-permute-start(f32[8,256]{1,0:T(8,128)S(1)} %stack.55), channel_id=1, source_target_pairs={{0,8},{4,12},{8,0},{12,4},{1,9},{5,13},{9,1},{13,5},{2,10},{6,14},... | collective-permute-start | bytes 24584 | tf_op jit(solution)/shard_map/ppermute | solution.py:69
  170.4 3.9 %collective-permute-start.5 = (f32[8,256]{1,0:T(8,128)S(1)}, f32[8,256]{1,0:T(8,128)S(1)}, u32[]{:S(2)}, u32[]{:S(2)}) collective-permute-start(f32[8,256]{1,0:T(8,128)S(1)} %stack.55), channel_id=1, source_target_pairs={{0,12},{4,0},{8,4},{12,8},{1,13},{5,1},{9,5},{13,9},{2,14},{6,2},{... | collective-permute-start | bytes 24584 | tf_op jit(solution)/shard_map/ppermute | solution.py:69
  176.3 2.2 copy-start.5
  180.7 4.1 %copy-start.1 = (bf16[1536,256]{1,0:T(8,128)(2,1)}, bf16[1536,256]{1,0:T(8,128)(2,1)S(1)}, u32[]{:S(2)}) copy-start(bf16[1536,256]{1,0:T(8,128)(2,1)S(1)} %fusion.24) | copy-start | bytes 2359300
  180.8 4.1 %copy-start.16 = (bf16[1280,256]{1,0:T(8,128)(2,1)S(1)}, bf16[1280,256]{1,0:T(8,128)(2,1)}, u32[]{:S(2)}) copy-start(bf16[1280,256]{1,0:T(8,128)(2,1)} %fusion.8) | copy-start | bytes 1966084
  186.0 110.0 %all-reduce.2.cloned.1.call-start = ((), (), s32[]{:S(2)}) async-start(), calls=%async_computation.6 | async-start | bytes 1310720 | tf_op jit(solution)/shard_map/psum | solution.py:182
  186.1 2.5 copy-start.2
  188.6 8.2 %collective-permute-start.16 = (bf16[1280,320]{0,1:T(8,128)(2,1)}, bf16[1280,320]{0,1:T(8,128)(2,1)}, u32[]{:S(2)}, u32[]{:S(2)}) collective-permute-start(bf16[1280,320]{0,1:T(8,128)(2,1)} %convolution_convert_fusion.4), channel_id=1, source_target_pairs={{0,1},{1,0},{2,3},{3,2},{4,5},{5,4},{6,7},{7,6},{8,9},{9,8},{10,11... | collective-permute-start | bytes 2457608 | tf_op jit(solution)/shard_map/ppermute | solution.py:109
  190.9 9.9 %collective-permute-start.7 = (bf16[1536,320]{0,1:T(8,128)(2,1)}, bf16[1536,320]{0,1:T(8,128)(2,1)}, u32[]{:S(2)}, u32[]{:S(2)}) collective-permute-start(bf16[1536,320]{0,1:T(8,128)(2,1)} %convolution_convert_fusion.2), channel_id=1, source_target_pairs={{0,1},{1,0},{2,3},{3,2},{4,5},{5,4},{6,7},{7,6},{8,9},{9,8},{10,11... | collective-permute-start | bytes 2949128 | tf_op jit(solution)/shard_map/ppermute | solution.py:109
  191.4 2.5 copy-start.3
  191.4 5.4 %copy-start.6 = (bf16[1280,256]{1,0:T(8,128)(2,1)S(1)}, bf16[1280,256]{1,0:T(8,128)(2,1)}, u32[]{:S(2)}) copy-start(bf16[1280,256]{1,0:T(8,128)(2,1)} %copy-done.5) | copy-start | bytes 1966084
  194.0 10.1 %collective-permute-start.15 = (bf16[1280,320]{0,1:T(8,128)(2,1)}, bf16[1280,320]{0,1:T(8,128)(2,1)}, u32[]{:S(2)}, u32[]{:S(2)}) collective-permute-start(bf16[1280,320]{0,1:T(8,128)(2,1)} %convolution_convert_fusion.5), channel_id=1, source_target_pairs={{0,1},{1,0},{2,3},{3,2},{4,5},{5,4},{6,7},{7,6},{8,9},{9,8},{10,11... | collective-permute-start | bytes 2457608 | tf_op jit(solution)/shard_map/ppermute | solution.py:110
  196.3 27.5 %collective-permute-start.6 = (bf16[1536,320]{0,1:T(8,128)(2,1)}, bf16[1536,320]{0,1:T(8,128)(2,1)}, u32[]{:S(2)}, u32[]{:S(2)}) collective-permute-start(bf16[1536,320]{0,1:T(8,128)(2,1)} %convolution_convert_fusion.3), channel_id=1, source_target_pairs={{0,1},{1,0},{2,3},{3,2},{4,5},{5,4},{6,7},{7,6},{8,9},{9,8},{10,11... | collective-permute-start | bytes 2949128 | tf_op jit(solution)/shard_map/ppermute | solution.py:110
  199.4 21.4 %collective-permute-start.17 = (bf16[1280,320]{0,1:T(8,128)(2,1)}, bf16[1280,320]{0,1:T(8,128)(2,1)}, u32[]{:S(2)}, u32[]{:S(2)}) collective-permute-start(bf16[1280,320]{0,1:T(8,128)(2,1)} %fusion.4), channel_id=1, source_target_pairs={{0,2},{2,0},{1,3},{3,1},{4,6},{6,4},{5,7},{7,5},{8,10},{10,8},{9,1... | collective-permute-start | bytes 2457608 | tf_op jit(solution)/shard_map/ppermute | solution.py:111
  203.5 37.4 %collective-permute-start.8 = (bf16[1536,320]{0,1:T(8,128)(2,1)}, bf16[1536,320]{0,1:T(8,128)(2,1)}, u32[]{:S(2)}, u32[]{:S(2)}) collective-permute-start(bf16[1536,320]{0,1:T(8,128)(2,1)} %fusion.5), channel_id=1, source_target_pairs={{0,2},{2,0},{1,3},{3,1},{4,6},{6,4},{5,7},{7,5},{8,10},{10,8},{9,1... | collective-permute-start | bytes 2949128 | tf_op jit(solution)/shard_map/ppermute | solution.py:111
  204.1 36.8 %copy-start.4 = (bf16[1536,256]{1,0:T(8,128)(2,1)S(1)}, bf16[1536,256]{1,0:T(8,128)(2,1)}, u32[]{:S(2)}) copy-start(bf16[1536,256]{1,0:T(8,128)(2,1)} %copy-done.1) | copy-start | bytes 2359300
  243.9 2.6 copy-start.8
  245.1 4.7 %copy-start.10 = (bf16[320,1280]{1,0:T(8,128)(2,1)S(1)}, bf16[320,1280]{1,0:T(8,128)(2,1)}, u32[]{:S(2)}) copy-start(bf16[320,1280]{1,0:T(8,128)(2,1)} %param.18) | copy-start | bytes 2457604
  246.5 5.8 %copy-start.9 = (bf16[320,256]{1,0:T(8,128)(2,1)}, bf16[320,256]{1,0:T(8,128)(2,1)S(1)}, u32[]{:S(2)}) copy-start(bf16[320,256]{1,0:T(8,128)(2,1)S(1)} %get-tuple-element.29) | copy-start | bytes 491524
  249.7 2.6 copy-start.12
  253.7 12.7 %copy-start.15 = (f32[320,320]{1,0:T(8,128)S(1)}, f32[320,320]{1,0:T(8,128)}, u32[]{:S(2)}) copy-start(f32[320,320]{1,0:T(8,128)} %fusion.65) | copy-start | bytes 1228804
  253.7 2.4 collective-permute-start.22
  253.8 7.1 %collective-permute-start.21 = (bf16[320,320]{1,0:T(8,128)(2,1)}, bf16[320,320]{1,0:T(8,128)(2,1)S(1)}, u32[]{:S(2)}, u32[]{:S(2)}) collective-permute-start(bf16[320,320]{1,0:T(8,128)(2,1)} %convolution_convert_fusion.9), channel_id=1, source_target_pairs={{0,1},{1,0},{2,3},{3,2},{4,5},{5,4},{6,7},{7,6},{8,9},{9,8},{10,11... | collective-permute-start | bytes 614408 | tf_op jit(solution)/shard_map/ppermute | solution.py:110
  254.3 4.7 %collective-permute-start.19 = (bf16[320,320]{1,0:T(8,128)(2,1)}, bf16[320,320]{1,0:T(8,128)(2,1)S(1)}, u32[]{:S(2)}, u32[]{:S(2)}) collective-permute-start(bf16[320,320]{1,0:T(8,128)(2,1)} %convolution_convert_fusion.10), channel_id=1, source_target_pairs={{0,1},{1,0},{2,3},{3,2},{4,5},{5,4},{6,7},{7,6},{8,9},{9,8},{10,11... | collective-permute-start | bytes 614408 | tf_op jit(solution)/shard_map/ppermute | solution.py:109
  254.4 12.8 %collective-permute-start.18 = (bf16[320,320]{1,0:T(8,128)(2,1)}, bf16[320,320]{1,0:T(8,128)(2,1)S(1)}, u32[]{:S(2)}, u32[]{:S(2)}) collective-permute-start(bf16[320,320]{1,0:T(8,128)(2,1)} %convolution_convert_fusion.11), channel_id=1, source_target_pairs={{0,1},{1,0},{2,3},{3,2},{4,5},{5,4},{6,7},{7,6},{8,9},{9,8},{10,11... | collective-permute-start | bytes 614408 | tf_op jit(solution)/shard_map/ppermute | solution.py:110
  257.5 8.9 %collective-permute-start.23 = (bf16[320,320]{1,0:T(8,128)(2,1)S(1)}, bf16[320,320]{1,0:T(8,128)(2,1)S(1)}, u32[]{:S(2)}, u32[]{:S(2)}) collective-permute-start(bf16[320,320]{1,0:T(8,128)(2,1)S(1)} %add_convert_fusion.1), channel_id=1, source_target_pairs={{0,2},{2,0},{1,3},{3,1},{4,6},{6,4},{5,7},{7,5},{8,10},{10,8},{9,1... | collective-permute-start | bytes 614408 | tf_op jit(solution)/shard_map/ppermute | solution.py:111
  260.3 10.4 %collective-permute-start.20 = (bf16[320,320]{1,0:T(8,128)(2,1)S(1)}, bf16[320,320]{1,0:T(8,128)(2,1)S(1)}, u32[]{:S(2)}, u32[]{:S(2)}) collective-permute-start(bf16[320,320]{1,0:T(8,128)(2,1)S(1)} %add_convert_fusion.3), channel_id=1, source_target_pairs={{0,2},{2,0},{1,3},{3,1},{4,6},{6,4},{5,7},{7,5},{8,10},{10,8},{9,1... | collective-permute-start | bytes 614408 | tf_op jit(solution)/shard_map/ppermute | solution.py:111
Sparse Core Ops, SparseCore 0:
  17.6 75.6 reduce-scatter.5
  95.6 65.7 reduce-scatter.3
  186.2 32.8 reduce-scatter.7
  253.8 42.1 all-reduce.1

commit v3 on v2

--- a/solution.py
+++ b/solution.py
@@ -91,7 +91,7 @@
     return full
 
 
-def summed_product(left, right):
+def summed_product(left, right, after=None):
     sections, cores = lax.axis_size("sec"), lax.axis_size("dp")
     if sections != 2 or cores != 2:
         product = jnp.dot(left, right, preferred_element_type=jnp.float32)
@@ -108,9 +108,10 @@
 
     far = lax.ppermute(piece(1 - sec, 1 - core).astype(jnp.bfloat16), "dp", swap)
     near = lax.ppermute(piece(sec, 1 - core).astype(jnp.bfloat16), "dp", swap)
-    other = lax.ppermute(
-        (piece(1 - sec, core) + far.astype(jnp.float32)).astype(jnp.bfloat16), "sec", swap
-    )
+    outgoing = (piece(1 - sec, core) + far.astype(jnp.float32)).astype(jnp.bfloat16)
+    if after is not None:
+        outgoing, _ = lax.optimization_barrier((outgoing, after))
+    other = lax.ppermute(outgoing, "sec", swap)
     total = piece(sec, core) + near.astype(jnp.float32) + other.astype(jnp.float32)
     return total.astype(jnp.bfloat16)
 
@@ -121,7 +122,7 @@
         "tp",
         scatter_dimension=0,
         tiled=True,
-    ).astype(jnp.float32)
+    )
 
 
 def local(
@@ -155,21 +156,21 @@
     giant_pred = lax.dot_general(
         giant_head, giant_hidden, CONTRACT_LAST, preferred_element_type=jnp.float32
     )
-    clip_stats = tp_sum(token_sums(clip_own, clip_gain, clip_pred))
-    clip_slope = make_slope(clip_own, clip_gain, clip_pred, clip_stats, clip_width)
+    clip_stats = tp_sum(token_sums(clip_own.astype(jnp.float32), clip_gain, clip_pred))
+    clip_slope = make_slope(clip_own.astype(jnp.float32), clip_gain, clip_pred, clip_stats, clip_width)
     clip_grad = summed_product(clip_slope, clip_hidden)
     clip_back = lax.dot_general(
         clip_head, clip_slope, CONTRACT_FIRST, preferred_element_type=jnp.float32
     ).astype(jnp.bfloat16)
-    giant_stats = tp_sum(token_sums(giant_own, giant_gain, giant_pred))
-    giant_slope = make_slope(giant_own, giant_gain, giant_pred, giant_stats, giant_width)
+    giant_own, clip_grad, clip_back = lax.optimization_barrier((giant_own, clip_grad, clip_back))
+    giant_stats = tp_sum(token_sums(giant_own.astype(jnp.float32), giant_gain, giant_pred))
+    giant_slope = make_slope(giant_own.astype(jnp.float32), giant_gain, giant_pred, giant_stats, giant_width)
     giant_back = lax.dot_general(
         giant_head, giant_slope, CONTRACT_FIRST, preferred_element_type=jnp.float32
     ).astype(jnp.bfloat16)
     back = lax.psum_scatter(
         jnp.concatenate((giant_back, clip_back), axis=1), "tp", scatter_dimension=0, tiled=True
     ).astype(jnp.float32)
-    giant_grad = summed_product(giant_slope, giant_hidden)
     tokens = student_features.shape[0]
     giant_pslope = (back[:, :tokens] * gelu_slope(giant_pre.T)).astype(jnp.bfloat16)
     clip_pslope = (back[:, tokens:] * gelu_slope(clip_pre.T)).astype(jnp.bfloat16)
@@ -179,7 +180,9 @@
     feature_term = feature_term + lax.dot_general(
         clip_pslope, clip_first, CONTRACT_FIRST, preferred_element_type=jnp.float32
     )
-    feature_sum = lax.psum(feature_term.astype(jnp.bfloat16), "tp")
+    feature_term = feature_term.astype(jnp.bfloat16)
+    feature_sum = lax.psum(feature_term, "tp")
+    giant_grad = summed_product(giant_slope, giant_hidden, after=feature_term)
     giant_first_grad = summed_product(giant_pslope, student_features)
     clip_first_grad = summed_product(clip_pslope, student_features)
     return (giant_grad, clip_grad, giant_first_grad, clip_first_grad, feature_sum)

time: 305 us -> 274 us (0.90)
  waiting for transfers between devices: 159 us -> 128 us
    reduce_scatter x1, waiting for transfers between devices: 0.01 us -> 26.8 us  [local(): lax.psum_scatter(jnp.concatenate((giant_back, clip_back), axis=1), 'tp',...]
    psum x1, waiting for transfers between devices: 24.6 us -> 0.01 us  [local(): feature_sum = lax.psum(feature_term, 'tp')]
    ppermute x4, waiting for transfers between devices: 42.8 us -> 26.3 us  [summed_product(): other = lax.ppermute(outgoing, 'sec', swap)]
    reduce_scatter x2, waiting for transfers between devices: 53.9 us -> 41.2 us  [own_rows(): lax.psum_scatter(project_teacher(weight_rows, context).astype(jnp.bfloat1...]
    ppermute x12, waiting for transfers between devices: 37.6 us -> 32.8 us  [tp_shift(): lax.ppermute(value, 'tp', [(i, (i + step) % count) for i in range(count)])]
    dot_general x16, matrix products: 30.2 us -> 27.1 us  [piece(): return jnp.dot(left, columns, preferred_element_type=jnp.float32)]
  transfers between devices with their start and end apart: 28 -> 28, of which waited for: 15 -> 13; matrix products, arithmetic and copies ran while one was open for 20% -> 26% of each run, Pallas kernels for 0% -> 0%
where the time goes in v3:
time: 274 us; the launch traced here: 273 us
  waiting for transfers between devices  128 us (47%)
  matrix products  70 us (26%)
  starting transfers between devices  34 us (12%)
  local copies, waits for them, and re-layouts  14.8 us (5%)
  between operations  14.2 us (5%)
  other arithmetic  12.4 us (5%)
    reduce_scatter x2, waiting for transfers between devices, own_rows(): lax.psum_scatter(project_teacher(weight_rows, context).astype(jnp.bfloat1...  41.2 us
    ppermute x12, waiting for transfers between devices, tp_shift(): lax.ppermute(value, 'tp', [(i, (i + step) % count) for i in range(count)])  32.8 us
    dot_general x16, matrix products, piece(): return jnp.dot(left, columns, preferred_element_type=jnp.float32)  27.1 us
    reduce_scatter x1, waiting for transfers between devices, local(): lax.psum_scatter(jnp.concatenate((giant_back, clip_back), axis=1), 'tp',...  26.8 us
    ppermute x12, starting transfers between devices, tp_shift(): lax.ppermute(value, 'tp', [(i, (i + step) % count) for i in range(count)])  26.7 us
    ppermute x4, waiting for transfers between devices, summed_product(): other = lax.ppermute(outgoing, 'sec', swap)  26.3 us
    dot_general x2, matrix products, project_teacher(): lax.dot_general(weight_rows, context, CONTRACT_FIRST, preferred_element_t...  20.8 us
    dynamic_update_slice x6, local copies, waits for them, and re-layouts, tp_columns(): lax.dynamic_update_slice_in_dim(full, part, (own - step) % count * share, 1)  9.55 us
  transfers between devices with their start and end apart: 28, of which 13 were waited for; matrix products, arithmetic and copies ran while one was open for 26% of the time, Pallas kernels for 0%

profile of v3, /device:TPU:0, one launch (start us, length us, event | category | flops | bytes accessed | tf_op | source)
XLA Modules:
  0.0 273.1 jit_solution(2651828932205807868)
XLA Ops:
  7.2 10.2 %convolution_convert_fusion.1 = bf16[5120,256]{1,0:T(8,128)(2,1)} fusion(bf16[1280,5120]{1,0:T(8,128)(2,1)} %param.14, bf16[1280,256]{1,0:T(8,128)(2,1)} %param.12), kind=kOutput, calls=%fused_computation.1 | convolution fusion | flops 3356753920 | bytes 16384000 | tf_op jit(solution)/shard_map/dot_general | solution.py:28
  17.5 10.6 %convolution_convert_fusion = bf16[6144,256]{1,0:T(8,128)(2,1)} fusion(bf16[1536,6144]{1,0:T(8,128)(2,1)} %param.13, bf16[1536,256]{1,0:T(8,128)(2,1)} %param.11), kind=kOutput, calls=%fused_computation | convolution fusion | flops 4833411072 | bytes 22806528 | tf_op jit(solution)/shard_map/dot_general | solution.py:28
  28.2 0.9 broadcast.85.clone
  29.1 2.6 constant_dynamic-update-slice_fusion.7
  31.7 3.0 %collective-permute-start = (bf16[256,320]{0,1:T(8,128)(2,1)S(1)}, bf16[256,320]{0,1:T(8,128)(2,1)}, u32[]{:S(2)}, u32[]{:S(2)}) collective-permute-start(bf16[256,320]{0,1:T(8,128)(2,1)S(1)} %get-tuple-element.36), channel_id=1, source_target_pairs={{0,4},{4,8},{8,12},{12,0},{1,5},{5,9},{9,13},{13,1},{2,6},{6,10},{... | collective-permute-start | bytes 491528 | tf_op jit(solution)/shard_map/ppermute | solution.py:69
  34.7 2.6 collective-permute-start.1
  37.3 1.3 collective-permute-start.2
  39.2 6.1 %collective-permute-done = bf16[256,320]{0,1:T(8,128)(2,1)} collective-permute-done((bf16[256,320]{0,1:T(8,128)(2,1)S(1)}, bf16[256,320]{0,1:T(8,128)(2,1)}, u32[]{:S(2)}, u32[]{:S(2)}) %collective-permute-start) | collective-permute-done | bytes 163872 | tf_op jit(solution)/shard_map/ppermute | solution.py:69
  45.4 1.6 constant_dynamic-update-slice_fusion.6
  47.0 9.8 %collective-permute-done.1 = bf16[256,320]{0,1:T(8,128)(2,1)} collective-permute-done((bf16[256,320]{0,1:T(8,128)(2,1)S(1)}, bf16[256,320]{0,1:T(8,128)(2,1)}, u32[]{:S(2)}, u32[]{:S(2)}) %collective-permute-start.1) | collective-permute-done | bytes 163872 | tf_op jit(solution)/shard_map/ppermute | solution.py:69
  56.7 1.6 constant_dynamic-update-slice_fusion.5
  58.3 1.6 constant_dynamic-update-slice_fusion.4
  59.9 22.9 %reduce-scatter.6.cloned.1.call-done = bf16[1280,256]{1,0:T(8,128)(2,1)} async-done(((bf16[5120,256]{1,0:T(8,128)(2,1)}), bf16[1280,256]{1,0:T(8,128)(2,1)}) %reduce-scatter.6.cloned.1.call-update) | async-done | bytes 655376 | tf_op jit(solution)/shard_map/reduce_scatter | solution.py:120
  82.8 3.7 %multiply_reduce_fusion.2 = (f32[256]{0:T(256)S(1)}, f32[256]{0:T(256)S(1)}, f32[256]{0:T(256)S(1)}, f32[256]{0:T(256)S(1)}, f32[256]{0:T(256)S(1)}, /*index=5*/...) fusion(f32[1280]{0:T(1024)S(1)} %copy-done.17, bf16[1280,256]{1,0:T(8,128)(2,1)} %reduce-scatter.6.cloned.1.call-done, ...), kind=kOutput, calls=%fused_computation.61 | convolution fusion | flops 843774208 | bytes 5910528 | tf_op jit(solution)/shard_map/dot_general | solution.py:153
  87.2 4.4 %collective-permute-start.3 = (f32[8,256]{1,0:T(8,128)S(1)}, f32[8,256]{1,0:T(8,128)S(1)}, u32[]{:S(2)}, u32[]{:S(2)}) collective-permute-start(f32[8,256]{1,0:T(8,128)S(1)} %stack.55), channel_id=1, source_target_pairs={{0,4},{4,8},{8,12},{12,0},{1,5},{5,9},{9,13},{13,1},{2,6},{6,10},{... | collective-permute-start | bytes 24584 | tf_op jit(solution)/shard_map/ppermute | solution.py:69
  91.6 2.8 %collective-permute-start.5 = (f32[8,256]{1,0:T(8,128)S(1)}, f32[8,256]{1,0:T(8,128)S(1)}, u32[]{:S(2)}, u32[]{:S(2)}) collective-permute-start(f32[8,256]{1,0:T(8,128)S(1)} %stack.55), channel_id=1, source_target_pairs={{0,12},{4,0},{8,4},{12,8},{1,13},{5,1},{9,5},{13,9},{2,14},{6,2},{... | collective-permute-start | bytes 24584 | tf_op jit(solution)/shard_map/ppermute | solution.py:69
  94.5 1.7 collective-permute-done.4
  96.3 1.9 fusion.34
  98.3 2.5 convolution_convert_fusion.4
  100.8 1.2 constant_dynamic-update-slice_fusion.3
  102.0 0.8 copy-done.13
  102.8 0.9 collective-permute-start.9
  103.7 2.5 convolution_convert_fusion.5
  106.5 2.5 fusion.4
  109.0 1.5 collective-permute-start.8
  110.5 3.6 %collective-permute-start.10 = (bf16[256,320]{0,1:T(8,128)(2,1)S(1)}, bf16[256,320]{0,1:T(8,128)(2,1)}, u32[]{:S(2)}, u32[]{:S(2)}) collective-permute-start(bf16[256,320]{0,1:T(8,128)(2,1)S(1)} %get-tuple-element.31), channel_id=1, source_target_pairs={{0,8},{4,12},{8,0},{12,4},{1,9},{5,13},{9,1},{13,5},{2,10},{6,14},... | collective-permute-start | bytes 491528 | tf_op jit(solution)/shard_map/ppermute | solution.py:69
  115.4 1.6 constant_dynamic-update-slice_fusion.2
  117.0 11.4 %collective-permute-done.10 = bf16[256,320]{0,1:T(8,128)(2,1)} collective-permute-done((bf16[256,320]{0,1:T(8,128)(2,1)S(1)}, bf16[256,320]{0,1:T(8,128)(2,1)}, u32[]{:S(2)}, u32[]{:S(2)}) %collective-permute-start.10) | collective-permute-done | bytes 163872 | tf_op jit(solution)/shard_map/ppermute | solution.py:69
  128.4 1.6 constant_dynamic-update-slice_fusion.1
  130.0 1.6 collective-permute-done.11
  131.7 1.6 constant_dynamic-update-slice_fusion
  133.3 3.4 %fusion.8 = bf16[1280,256]{1,0:T(8,128)(2,1)} fusion(bf16[1280,256]{1,0:T(8,128)(2,1)} %copy-done.4, bf16[1280,1280]{1,0:T(8,128)(2,1)S(1)} %copy-done), kind=kOutput, calls=%fused_computation.27 | convolution fusion | flops 839188480 | bytes 4587520 | tf_op jit(solution)/shard_map/dot_general | solution.py:162
  136.7 2.8 %fusion.3 = bf16[1280,320]{0,1:T(8,128)(2,1)} fusion(bf16[1280,256]{1,0:T(8,128)(2,1)S(1)} %copy-done.6, bf16[1280,320]{0,1:T(8,128)(2,1)} %collective-permute-done.8, bf16[1280,320]{0,1:T(8,128)(2,1)} %collective-permute-done.6, bf16[256,1280]{0,1:T(8,128)(2,1)} %constant_dynamic-update-slice_fusion.4, s32[]{:T(128)S(6)} %select_n.108), kind=kOutput, calls=%fused_computation.18 | convolution fusion | flops 211763200 | bytes 3276804 | tf_op jit(solution)/shard_map/dot_general | solution.py:107
  139.5 18.3 %reduce-scatter.4.cloned.1.call-done = bf16[1536,256]{1,0:T(8,128)(2,1)} async-done(((bf16[6144,256]{1,0:T(8,128)(2,1)}), bf16[1536,256]{1,0:T(8,128)(2,1)}) %reduce-scatter.4.cloned.1.call-update) | async-done | bytes 786448 | tf_op jit(solution)/shard_map/reduce_scatter | solution.py:120
  157.8 5.3 %multiply_reduce_fusion = (f32[256]{0:T(256)S(1)}, f32[256]{0:T(256)S(1)}, f32[256]{0:T(256)S(1)}, f32[256]{0:T(256)S(1)}, f32[256]{0:T(256)S(1)}, /*index=5*/f3...) fusion(f32[1536]{0:T(1024)S(1)} %copy-done.18, bf16[1536,256]{1,0:T(8,128)(2,1)} %reduce-scatter.4.cloned.1.call-done, ...), kind=kOutput, calls=%fused_computation.48 | convolution fusion | flops 1012529408 | bytes 6960128 | tf_op jit(solution)/shard_map/dot_general | solution.py:156
  163.7 4.9 %collective-permute-start.12 = (f32[8,256]{1,0:T(8,128)S(1)}, f32[8,256]{1,0:T(8,128)S(1)}, u32[]{:S(2)}, u32[]{:S(2)}) collective-permute-start(f32[8,256]{1,0:T(8,128)S(1)} %stack.63), channel_id=1, source_target_pairs={{0,4},{4,8},{8,12},{12,0},{1,5},{5,9},{9,13},{13,1},{2,6},{6,10},{... | collective-permute-start | bytes 24584 | tf_op jit(solution)/shard_map/ppermute | solution.py:69
  168.6 2.8 %collective-permute-start.14 = (f32[8,256]{1,0:T(8,128)S(1)}, f32[8,256]{1,0:T(8,128)S(1)}, u32[]{:S(2)}, u32[]{:S(2)}) collective-permute-start(f32[8,256]{1,0:T(8,128)S(1)} %stack.63), channel_id=1, source_target_pairs={{0,12},{4,0},{8,4},{12,8},{1,13},{5,1},{9,5},{13,9},{2,14},{6,2},{... | collective-permute-start | bytes 24584 | tf_op jit(solution)/shard_map/ppermute | solution.py:69
  171.5 1.7 collective-permute-done.13
  173.3 2.1 fusion.24
  175.4 4.1 %fusion.7 = bf16[1280,256]{1,0:T(8,128)(2,1)S(1)} fusion(bf16[1536,256]{1,0:T(8,128)(2,1)S(1)} %fusion.24, bf16[1536,1280]{1,0:T(8,128)(2,1)} %param.20), kind=kOutput, calls=%fused_computation.26 | convolution fusion | flops 1006960640 | bytes 5373952 | tf_op jit(solution)/shard_map/dot_general | solution.py:168
  179.5 1.2 pad_maximum_fusion
  180.8 1.7 convolution_convert_fusion.2
  182.6 1.4 convolution_convert_fusion.3
  185.1 1.4 fusion.5
  186.5 26.8 %reduce-scatter.8.cloned.1.call-done = bf16[320,512]{1,0:T(8,128)(2,1)} async-done(((bf16[1280,512]{1,0:T(8,128)(2,1)}), bf16[320,512]{1,0:T(8,128)(2,1)}) %reduce-scatter.8.cloned.1.call-update) | async-done | bytes 327696 | tf_op jit(solution)/shard_map/reduce_scatter | solution.py:171
  213.3 1.1 convert_element_type.158
  214.5 1.3 fusion.46
  215.8 1.0 convolution_convert_fusion.8
  216.9 1.1 convolution_convert_fusion.9
  217.9 1.1 fusion.65
  219.0 1.0 convolution_convert_fusion.10
  220.1 1.0 convolution_convert_fusion.11
  222.7 1.4 fusion.6
  224.1 1.3 fusion.67
  225.5 1.5 collective-permute-start.17
  227.0 1.4 add_convert_fusion.1
  229.1 1.4 add_convert_fusion.3
  230.5 1.5 collective-permute-start.20
  232.0 23.6 %collective-permute-done.23 = bf16[320,320]{1,0:T(8,128)(2,1)S(1)} collective-permute-done((bf16[320,320]{1,0:T(8,128)(2,1)S(1)}, bf16[320,320]{1,0:T(8,128)(2,1)S(1)}, u32[]{:S(2)}, u32[]{:S(2)}) %collective-permute-start.23) | collective-permute-done | bytes 204832 | tf_op jit(solution)/shard_map/ppermute | solution.py:114
  255.7 1.7 add_convert_fusion
  257.4 2.6 collective-permute-done.20
  260.1 1.7 add_convert_fusion.2
  261.8 2.8 %fusion.2 = bf16[1536,320]{0,1:T(8,128)(2,1)} fusion(bf16[1536,256]{1,0:T(8,128)(2,1)S(1)} %copy-done.3, bf16[1536,320]{0,1:T(8,128)(2,1)S(1)} %collective-permute-done.17, bf16[1536,320]{0,1:T(8,128)(2,1)} %collective-permute-done.15, bf16[256,1280]{0,1:T(8,128)(2,1)} %constant_dynamic-update-slice_fusion, s32[]{:T(128)S(6)} %select_n.108), kind=kOutput, calls=%fused_computation.15 | convolution fusion | flops 254115840 | bytes 3899396 | tf_op jit(solution)/shard_map/dot_general | solution.py:107
  264.6 2.0 copy.47
  (98 shorter events, 7.5 us)
Async XLA Ops:
  7.2 75.7 %copy-start = (bf16[1280,1280]{1,0:T(8,128)(2,1)S(1)}, bf16[1280,1280]{1,0:T(8,128)(2,1)}, u32[]{:S(2)}) copy-start(bf16[1280,1280]{1,0:T(8,128)(2,1)} %param.21) | copy-start | bytes 9830404
  7.2 75.6 %reduce-scatter.6.cloned.1.call-start = ((), (), s32[]{:S(2)}) async-start(), calls=%async_computation.4 | async-start | bytes 3276800 | tf_op jit(solution)/shard_map/reduce_scatter | solution.py:120
  17.5 140.3 %reduce-scatter.4.cloned.1.call-start = ((), (), s32[]{:S(2)}) async-start(), calls=%async_computation.3 | async-start | bytes 3932160 | tf_op jit(solution)/shard_map/reduce_scatter | solution.py:120
  28.2 10.5 %copy-start.17 = (f32[1280]{0:T(1024)S(1)}, f32[1280]{0:T(1024)}, u32[]{:S(2)}) copy-start(f32[1280]{0:T(1024)} %param.16) | copy-start | bytes 15364
  28.2 185.2 %reduce-scatter.8.cloned.1.call-start = ((), (), s32[]{:S(2)}) async-start(), calls=%async_computation.5 | async-start | bytes 1638400 | tf_op jit(solution)/shard_map/reduce_scatter | solution.py:171
  31.7 13.7 %collective-permute-start = (bf16[256,320]{0,1:T(8,128)(2,1)S(1)}, bf16[256,320]{0,1:T(8,128)(2,1)}, u32[]{:S(2)}, u32[]{:S(2)}) collective-permute-start(bf16[256,320]{0,1:T(8,128)(2,1)S(1)} %get-tuple-element.36), channel_id=1, source_target_pairs={{0,4},{4,8},{8,12},{12,0},{1,5},{5,9},{9,13},{13,1},{2,6},{6,10},{... | collective-permute-start | bytes 491528 | tf_op jit(solution)/shard_map/ppermute | solution.py:69
  34.7 22.0 %collective-permute-start.1 = (bf16[256,320]{0,1:T(8,128)(2,1)S(1)}, bf16[256,320]{0,1:T(8,128)(2,1)}, u32[]{:S(2)}, u32[]{:S(2)}) collective-permute-start(bf16[256,320]{0,1:T(8,128)(2,1)S(1)} %get-tuple-element.36), channel_id=1, source_target_pairs={{0,8},{4,12},{8,0},{12,4},{1,9},{5,13},{9,1},{13,5},{2,10},{6,14},... | collective-permute-start | bytes 491528 | tf_op jit(solution)/shard_map/ppermute | solution.py:69
  37.3 21.0 %collective-permute-start.2 = (bf16[256,320]{0,1:T(8,128)(2,1)S(1)}, bf16[256,320]{0,1:T(8,128)(2,1)}, u32[]{:S(2)}, u32[]{:S(2)}) collective-permute-start(bf16[256,320]{0,1:T(8,128)(2,1)S(1)} %get-tuple-element.36), channel_id=1, source_target_pairs={{0,12},{4,0},{8,4},{12,8},{1,13},{5,1},{9,5},{13,9},{2,14},{6,2},{... | collective-permute-start | bytes 491528 | tf_op jit(solution)/shard_map/ppermute | solution.py:69
  87.2 7.3 %collective-permute-start.3 = (f32[8,256]{1,0:T(8,128)S(1)}, f32[8,256]{1,0:T(8,128)S(1)}, u32[]{:S(2)}, u32[]{:S(2)}) collective-permute-start(f32[8,256]{1,0:T(8,128)S(1)} %stack.55), channel_id=1, source_target_pairs={{0,4},{4,8},{8,12},{12,0},{1,5},{5,9},{9,13},{13,1},{2,6},{6,10},{... | collective-permute-start | bytes 24584 | tf_op jit(solution)/shard_map/ppermute | solution.py:69
  91.6 4.7 %collective-permute-start.4 = (f32[8,256]{1,0:T(8,128)S(1)}, f32[8,256]{1,0:T(8,128)S(1)}, u32[]{:S(2)}, u32[]{:S(2)}) collective-permute-start(f32[8,256]{1,0:T(8,128)S(1)} %stack.55), channel_id=1, source_target_pairs={{0,8},{4,12},{8,0},{12,4},{1,9},{5,13},{9,1},{13,5},{2,10},{6,14},... | collective-permute-start | bytes 24584 | tf_op jit(solution)/shard_map/ppermute | solution.py:69
  91.6 4.6 %collective-permute-start.5 = (f32[8,256]{1,0:T(8,128)S(1)}, f32[8,256]{1,0:T(8,128)S(1)}, u32[]{:S(2)}, u32[]{:S(2)}) collective-permute-start(f32[8,256]{1,0:T(8,128)S(1)} %stack.55), channel_id=1, source_target_pairs={{0,12},{4,0},{8,4},{12,8},{1,13},{5,1},{9,5},{13,9},{2,14},{6,2},{... | collective-permute-start | bytes 24584 | tf_op jit(solution)/shard_map/ppermute | solution.py:69
  98.2 3.8 %copy-start.4 = (bf16[1280,256]{1,0:T(8,128)(2,1)}, bf16[1280,256]{1,0:T(8,128)(2,1)S(1)}, u32[]{:S(2)}) copy-start(bf16[1280,256]{1,0:T(8,128)(2,1)S(1)} %fusion.34) | copy-start | bytes 1966084
  98.2 2.6 copy-start.7
  98.3 2.6 copy-start.10
  100.7 5.7 %collective-permute-start.7 = (bf16[1280,320]{0,1:T(8,128)(2,1)}, bf16[1280,320]{0,1:T(8,128)(2,1)}, u32[]{:S(2)}, u32[]{:S(2)}) collective-permute-start(bf16[1280,320]{0,1:T(8,128)(2,1)} %convolution_convert_fusion.4), channel_id=1, source_target_pairs={{0,1},{1,0},{2,3},{3,2},{4,5},{5,4},{6,7},{7,6},{8,9},{9,8},{10,11... | collective-permute-start | bytes 2457608 | tf_op jit(solution)/shard_map/ppermute | solution.py:109
  102.0 0.8 copy-start.13
  102.8 12.6 %collective-permute-start.9 = (bf16[256,320]{0,1:T(8,128)(2,1)S(1)}, bf16[256,320]{0,1:T(8,128)(2,1)}, u32[]{:S(2)}, u32[]{:S(2)}) collective-permute-start(bf16[256,320]{0,1:T(8,128)(2,1)S(1)} %get-tuple-element.31), channel_id=1, source_target_pairs={{0,4},{4,8},{8,12},{12,0},{1,5},{5,9},{9,13},{13,1},{2,6},{6,10},{... | collective-permute-start | bytes 491528 | tf_op jit(solution)/shard_map/ppermute | solution.py:69
  103.7 2.8 %copy-start.5 = (bf16[1280,256]{1,0:T(8,128)(2,1)S(1)}, bf16[1280,256]{1,0:T(8,128)(2,1)}, u32[]{:S(2)}) copy-start(bf16[1280,256]{1,0:T(8,128)(2,1)} %copy-done.4) | copy-start | bytes 1966084
  106.2 8.2 %copy-start.18 = (f32[1536]{0:T(1024)S(1)}, f32[1536]{0:T(1024)}, u32[]{:S(2)}) copy-start(f32[1536]{0:T(1024)} %param.15) | copy-start | bytes 18436
  106.2 30.4 %collective-permute-start.6 = (bf16[1280,320]{0,1:T(8,128)(2,1)}, bf16[1280,320]{0,1:T(8,128)(2,1)}, u32[]{:S(2)}, u32[]{:S(2)}) collective-permute-start(bf16[1280,320]{0,1:T(8,128)(2,1)} %convolution_convert_fusion.5), channel_id=1, source_target_pairs={{0,1},{1,0},{2,3},{3,2},{4,5},{5,4},{6,7},{7,6},{8,9},{9,8},{10,11... | collective-permute-start | bytes 2457608 | tf_op jit(solution)/shard_map/ppermute | solution.py:110
  109.0 27.6 %collective-permute-start.8 = (bf16[1280,320]{0,1:T(8,128)(2,1)}, bf16[1280,320]{0,1:T(8,128)(2,1)}, u32[]{:S(2)}, u32[]{:S(2)}) collective-permute-start(bf16[1280,320]{0,1:T(8,128)(2,1)} %fusion.4), channel_id=1, source_target_pairs={{0,2},{2,0},{1,3},{3,1},{4,6},{6,4},{5,7},{7,5},{8,10},{10,8},{9,1... | collective-permute-start | bytes 2457608 | tf_op jit(solution)/shard_map/ppermute | solution.py:114
  110.5 18.0 %collective-permute-start.10 = (bf16[256,320]{0,1:T(8,128)(2,1)S(1)}, bf16[256,320]{0,1:T(8,128)(2,1)}, u32[]{:S(2)}, u32[]{:S(2)}) collective-permute-start(bf16[256,320]{0,1:T(8,128)(2,1)S(1)} %get-tuple-element.31), channel_id=1, source_target_pairs={{0,8},{4,12},{8,0},{12,4},{1,9},{5,13},{9,1},{13,5},{2,10},{6,14},... | collective-permute-start | bytes 491528 | tf_op jit(solution)/shard_map/ppermute | solution.py:69
  114.1 17.6 %collective-permute-start.11 = (bf16[256,320]{0,1:T(8,128)(2,1)S(1)}, bf16[256,320]{0,1:T(8,128)(2,1)}, u32[]{:S(2)}, u32[]{:S(2)}) collective-permute-start(bf16[256,320]{0,1:T(8,128)(2,1)S(1)} %get-tuple-element.31), channel_id=1, source_target_pairs={{0,12},{4,0},{8,4},{12,8},{1,13},{5,1},{9,5},{13,9},{2,14},{6,2},{... | collective-permute-start | bytes 491528 | tf_op jit(solution)/shard_map/ppermute | solution.py:69
  133.3 3.4 %copy-start.6 = (bf16[1280,256]{1,0:T(8,128)(2,1)S(1)}, bf16[1280,256]{1,0:T(8,128)(2,1)}, u32[]{:S(2)}) copy-start(bf16[1280,256]{1,0:T(8,128)(2,1)} %copy-done.4) | copy-start | bytes 1966084
  163.7 7.8 %collective-permute-start.12 = (f32[8,256]{1,0:T(8,128)S(1)}, f32[8,256]{1,0:T(8,128)S(1)}, u32[]{:S(2)}, u32[]{:S(2)}) collective-permute-start(f32[8,256]{1,0:T(8,128)S(1)} %stack.63), channel_id=1, source_target_pairs={{0,4},{4,8},{8,12},{12,0},{1,5},{5,9},{9,13},{13,1},{2,6},{6,10},{... | collective-permute-start | bytes 24584 | tf_op jit(solution)/shard_map/ppermute | solution.py:69
  168.6 4.5 %collective-permute-start.13 = (f32[8,256]{1,0:T(8,128)S(1)}, f32[8,256]{1,0:T(8,128)S(1)}, u32[]{:S(2)}, u32[]{:S(2)}) collective-permute-start(f32[8,256]{1,0:T(8,128)S(1)} %stack.63), channel_id=1, source_target_pairs={{0,8},{4,12},{8,0},{12,4},{1,9},{5,13},{9,1},{13,5},{2,10},{6,14},... | collective-permute-start | bytes 24584 | tf_op jit(solution)/shard_map/ppermute | solution.py:69
  168.6 4.6 %collective-permute-start.14 = (f32[8,256]{1,0:T(8,128)S(1)}, f32[8,256]{1,0:T(8,128)S(1)}, u32[]{:S(2)}, u32[]{:S(2)}) collective-permute-start(f32[8,256]{1,0:T(8,128)S(1)} %stack.63), channel_id=1, source_target_pairs={{0,12},{4,0},{8,4},{12,8},{1,13},{5,1},{9,5},{13,9},{2,14},{6,2},{... | collective-permute-start | bytes 24584 | tf_op jit(solution)/shard_map/ppermute | solution.py:69
  175.4 4.1 %copy-start.1 = (bf16[1536,256]{1,0:T(8,128)(2,1)}, bf16[1536,256]{1,0:T(8,128)(2,1)S(1)}, u32[]{:S(2)}) copy-start(bf16[1536,256]{1,0:T(8,128)(2,1)S(1)} %fusion.24) | copy-start | bytes 2359300
  175.4 4.1 %copy-start.16 = (bf16[1280,256]{1,0:T(8,128)(2,1)S(1)}, bf16[1280,256]{1,0:T(8,128)(2,1)}, u32[]{:S(2)}) copy-start(bf16[1280,256]{1,0:T(8,128)(2,1)} %fusion.8) | copy-start | bytes 1966084
  180.7 83.9 %all-reduce.2.cloned.1.call-start = ((), (), s32[]{:S(2)}) async-start(), calls=%async_computation.6 | async-start | bytes 1310720 | tf_op jit(solution)/shard_map/psum | solution.py:184
  180.7 1.8 copy-start.2
  180.7 1.8 copy-start.14
  182.5 2.6 collective-permute-start.16
  184.0 77.8 %collective-permute-start.15 = (bf16[1536,320]{0,1:T(8,128)(2,1)}, bf16[1536,320]{0,1:T(8,128)(2,1)}, u32[]{:S(2)}, u32[]{:S(2)}) collective-permute-start(bf16[1536,320]{0,1:T(8,128)(2,1)} %convolution_convert_fusion.3), channel_id=1, source_target_pairs={{0,1},{1,0},{2,3},{3,2},{4,5},{5,4},{6,7},{7,6},{8,9},{9,8},{10,11... | collective-permute-start | bytes 2949128 | tf_op jit(solution)/shard_map/ppermute | solution.py:110
  213.3 2.5 copy-start.8
  215.8 6.9 %copy-start.9 = (bf16[320,256]{1,0:T(8,128)(2,1)}, bf16[320,256]{1,0:T(8,128)(2,1)S(1)}, u32[]{:S(2)}) copy-start(bf16[320,256]{1,0:T(8,128)(2,1)S(1)} %get-tuple-element.37) | copy-start | bytes 491524
  215.8 5.3 %copy-start.11 = (bf16[320,1280]{1,0:T(8,128)(2,1)S(1)}, bf16[320,1280]{1,0:T(8,128)(2,1)}, u32[]{:S(2)}) copy-start(bf16[320,1280]{1,0:T(8,128)(2,1)} %param.18) | copy-start | bytes 2457604
  220.1 2.7 copy-start.12
  221.6 3.9 %collective-permute-start.22 = (bf16[320,320]{1,0:T(8,128)(2,1)}, bf16[320,320]{1,0:T(8,128)(2,1)}, u32[]{:S(2)}, u32[]{:S(2)}) collective-permute-start(bf16[320,320]{1,0:T(8,128)(2,1)} %convolution_convert_fusion.8), channel_id=1, source_target_pairs={{0,1},{1,0},{2,3},{3,2},{4,5},{5,4},{6,7},{7,6},{8,9},{9,8},{10,11... | collective-permute-start | bytes 614408 | tf_op jit(solution)/shard_map/ppermute | solution.py:109
  221.7 8.8 %collective-permute-start.21 = (bf16[320,320]{1,0:T(8,128)(2,1)}, bf16[320,320]{1,0:T(8,128)(2,1)}, u32[]{:S(2)}, u32[]{:S(2)}) collective-permute-start(bf16[320,320]{1,0:T(8,128)(2,1)} %convolution_convert_fusion.9), channel_id=1, source_target_pairs={{0,1},{1,0},{2,3},{3,2},{4,5},{5,4},{6,7},{7,6},{8,9},{9,8},{10,11... | collective-permute-start | bytes 614408 | tf_op jit(solution)/shard_map/ppermute | solution.py:110
  222.2 6.3 %collective-permute-start.19 = (bf16[320,320]{1,0:T(8,128)(2,1)}, bf16[320,320]{1,0:T(8,128)(2,1)}, u32[]{:S(2)}, u32[]{:S(2)}) collective-permute-start(bf16[320,320]{1,0:T(8,128)(2,1)} %convolution_convert_fusion.10), channel_id=1, source_target_pairs={{0,1},{1,0},{2,3},{3,2},{4,5},{5,4},{6,7},{7,6},{8,9},{9,8},{10,11... | collective-permute-start | bytes 614408 | tf_op jit(solution)/shard_map/ppermute | solution.py:109
  222.3 35.1 %collective-permute-start.18 = (bf16[320,320]{1,0:T(8,128)(2,1)}, bf16[320,320]{1,0:T(8,128)(2,1)}, u32[]{:S(2)}, u32[]{:S(2)}) collective-permute-start(bf16[320,320]{1,0:T(8,128)(2,1)} %convolution_convert_fusion.11), channel_id=1, source_target_pairs={{0,1},{1,0},{2,3},{3,2},{4,5},{5,4},{6,7},{7,6},{8,9},{9,8},{10,11... | collective-permute-start | bytes 614408 | tf_op jit(solution)/shard_map/ppermute | solution.py:110
  224.1 31.5 %copy-start.15 = (f32[320,320]{1,0:T(8,128)S(1)}, f32[320,320]{1,0:T(8,128)}, u32[]{:S(2)}) copy-start(f32[320,320]{1,0:T(8,128)} %fusion.65) | copy-start | bytes 1228804
  225.5 36.3 %collective-permute-start.17 = (bf16[1536,320]{0,1:T(8,128)(2,1)}, bf16[1536,320]{0,1:T(8,128)(2,1)S(1)}, u32[]{:S(2)}, u32[]{:S(2)}) collective-permute-start(bf16[1536,320]{0,1:T(8,128)(2,1)} %fusion.5), channel_id=1, source_target_pairs={{0,2},{2,0},{1,3},{3,1},{4,6},{6,4},{5,7},{7,5},{8,10},{10,8},{9,1... | collective-permute-start | bytes 2949128 | tf_op jit(solution)/shard_map/ppermute | solution.py:114
  228.5 33.3 %copy-start.3 = (bf16[1536,256]{1,0:T(8,128)(2,1)S(1)}, bf16[1536,256]{1,0:T(8,128)(2,1)}, u32[]{:S(2)}) copy-start(bf16[1536,256]{1,0:T(8,128)(2,1)} %copy-done.1) | copy-start | bytes 2359300
  228.5 27.2 %collective-permute-start.23 = (bf16[320,320]{1,0:T(8,128)(2,1)S(1)}, bf16[320,320]{1,0:T(8,128)(2,1)S(1)}, u32[]{:S(2)}, u32[]{:S(2)}) collective-permute-start(bf16[320,320]{1,0:T(8,128)(2,1)S(1)} %add_convert_fusion.1), channel_id=1, source_target_pairs={{0,2},{2,0},{1,3},{3,1},{4,6},{6,4},{5,7},{7,5},{8,10},{10,8},{9,1... | collective-permute-start | bytes 614408 | tf_op jit(solution)/shard_map/ppermute | solution.py:114
  230.5 29.5 %collective-permute-start.20 = (bf16[320,320]{1,0:T(8,128)(2,1)S(1)}, bf16[320,320]{1,0:T(8,128)(2,1)S(1)}, u32[]{:S(2)}, u32[]{:S(2)}) collective-permute-start(bf16[320,320]{1,0:T(8,128)(2,1)S(1)} %add_convert_fusion.3), channel_id=1, source_target_pairs={{0,2},{2,0},{1,3},{3,1},{4,6},{6,4},{5,7},{7,5},{8,10},{10,8},{9,1... | collective-permute-start | bytes 614408 | tf_op jit(solution)/shard_map/ppermute | solution.py:114
Sparse Core Ops, SparseCore 0:
  17.6 65.1 reduce-scatter.5
  85.1 72.5 reduce-scatter.3
  180.8 32.4 reduce-scatter.7
  224.3 39.2 all-reduce.1

commit v4 on v3

--- a/solution.py
+++ b/solution.py
@@ -163,17 +163,19 @@
         clip_head, clip_slope, CONTRACT_FIRST, preferred_element_type=jnp.float32
     ).astype(jnp.bfloat16)
     giant_own, clip_grad, clip_back = lax.optimization_barrier((giant_own, clip_grad, clip_back))
+    clip_hslope = lax.psum_scatter(
+        clip_back, "tp", scatter_dimension=0, tiled=True
+    ).astype(jnp.float32)
     giant_stats = tp_sum(token_sums(giant_own.astype(jnp.float32), giant_gain, giant_pred))
     giant_slope = make_slope(giant_own.astype(jnp.float32), giant_gain, giant_pred, giant_stats, giant_width)
     giant_back = lax.dot_general(
         giant_head, giant_slope, CONTRACT_FIRST, preferred_element_type=jnp.float32
     ).astype(jnp.bfloat16)
-    back = lax.psum_scatter(
-        jnp.concatenate((giant_back, clip_back), axis=1), "tp", scatter_dimension=0, tiled=True
+    giant_hslope = lax.psum_scatter(
+        giant_back, "tp", scatter_dimension=0, tiled=True
     ).astype(jnp.float32)
-    tokens = student_features.shape[0]
-    giant_pslope = (back[:, :tokens] * gelu_slope(giant_pre.T)).astype(jnp.bfloat16)
-    clip_pslope = (back[:, tokens:] * gelu_slope(clip_pre.T)).astype(jnp.bfloat16)
+    giant_pslope = (giant_hslope * gelu_slope(giant_pre.T)).astype(jnp.bfloat16)
+    clip_pslope = (clip_hslope * gelu_slope(clip_pre.T)).astype(jnp.bfloat16)
     feature_term = lax.dot_general(
         giant_pslope, giant_first, CONTRACT_FIRST, preferred_element_type=jnp.float32
     )

time: 274 us -> 272 us (level)
  waiting for transfers between devices: 128 us -> 121 us
  matrix products: 70 us -> 76.1 us
    dot_general x16, matrix products: 27.1 us -> 33.6 us  [piece(): return jnp.dot(left, columns, preferred_element_type=jnp.float32)]
    reduce_scatter x1 -> x2, waiting for transfers between devices: 26.8 us -> 21.8 us  [the longest x1 15.5 us: local(): lax.psum_scatter(giant_back, 'tp', scatter_dimension=0, tiled=True)]
    ppermute x4, waiting for transfers between devices: 26.3 us -> 21.9 us  [summed_product(): other = lax.ppermute(outgoing, 'sec', swap)]
    psum x1, waiting for transfers between devices: 0.01 us -> 3.87 us  [local(): feature_sum = lax.psum(feature_term, 'tp')]
  transfers between devices with their start and end apart: 28 -> 29, of which waited for: 13 -> 14; matrix products, arithmetic and copies ran while one was open for 26% -> 30% of each run, Pallas kernels for 0% -> 0%
where the time goes in v4:
time: 272 us; the launch traced here: 271 us
  waiting for transfers between devices  121 us (44%)
  matrix products  76.1 us (28%)
  starting transfers between devices  34 us (12%)
  local copies, waits for them, and re-layouts  14.7 us (5%)
  between operations  14.1 us (5%)
  other arithmetic  10.4 us (4%)
    reduce_scatter x2, waiting for transfers between devices, own_rows(): lax.psum_scatter(project_teacher(weight_rows, context).astype(jnp.bfloat1...  41.1 us
    dot_general x16, matrix products, piece(): return jnp.dot(left, columns, preferred_element_type=jnp.float32)  33.6 us
    ppermute x12, waiting for transfers between devices, tp_shift(): lax.ppermute(value, 'tp', [(i, (i + step) % count) for i in range(count)])  32.7 us
    ppermute x12, starting transfers between devices, tp_shift(): lax.ppermute(value, 'tp', [(i, (i + step) % count) for i in range(count)])  26.7 us
    ppermute x4, waiting for transfers between devices, summed_product(): other = lax.ppermute(outgoing, 'sec', swap)  21.9 us
    dot_general x2, matrix products, project_teacher(): lax.dot_general(weight_rows, context, CONTRACT_FIRST, preferred_element_t...  20.8 us
    reduce_scatter x1, waiting for transfers between devices, local(): lax.psum_scatter(giant_back, 'tp', scatter_dimension=0, tiled=True)  15.5 us
    dynamic_update_slice x6, local copies, waits for them, and re-layouts, tp_columns(): lax.dynamic_update_slice_in_dim(full, part, (own - step) % count * share, 1)  9.55 us
  transfers between devices with their start and end apart: 29, of which 14 were waited for; matrix products, arithmetic and copies ran while one was open for 30% of the time, Pallas kernels for 0%

profile of v4, /device:TPU:0, one launch (start us, length us, event | category | flops | bytes accessed | tf_op | source)
XLA Modules:
  0.0 270.8 jit_solution(6243712514680685097)
XLA Ops:
  7.2 10.2 %convolution_convert_fusion.1 = bf16[5120,256]{1,0:T(8,128)(2,1)} fusion(bf16[1280,5120]{1,0:T(8,128)(2,1)} %param.14, bf16[1280,256]{1,0:T(8,128)(2,1)} %param.12), kind=kOutput, calls=%fused_computation.1 | convolution fusion | flops 3356753920 | bytes 16384000 | tf_op jit(solution)/shard_map/dot_general | solution.py:28
  17.5 10.6 %convolution_convert_fusion = bf16[6144,256]{1,0:T(8,128)(2,1)} fusion(bf16[1536,6144]{1,0:T(8,128)(2,1)} %param.13, bf16[1536,256]{1,0:T(8,128)(2,1)} %param.11), kind=kOutput, calls=%fused_computation | convolution fusion | flops 4833411072 | bytes 22806528 | tf_op jit(solution)/shard_map/dot_general | solution.py:28
  28.2 0.9 broadcast.85.clone
  29.1 2.6 constant_dynamic-update-slice_fusion.7
  31.7 3.0 %collective-permute-start = (bf16[256,320]{0,1:T(8,128)(2,1)S(1)}, bf16[256,320]{0,1:T(8,128)(2,1)}, u32[]{:S(2)}, u32[]{:S(2)}) collective-permute-start(bf16[256,320]{0,1:T(8,128)(2,1)S(1)} %get-tuple-element.36), channel_id=1, source_target_pairs={{0,4},{4,8},{8,12},{12,0},{1,5},{5,9},{9,13},{13,1},{2,6},{6,10},{... | collective-permute-start | bytes 491528 | tf_op jit(solution)/shard_map/ppermute | solution.py:69
  34.7 2.6 collective-permute-start.1
  37.3 1.3 collective-permute-start.2
  39.2 6.1 %collective-permute-done = bf16[256,320]{0,1:T(8,128)(2,1)} collective-permute-done((bf16[256,320]{0,1:T(8,128)(2,1)S(1)}, bf16[256,320]{0,1:T(8,128)(2,1)}, u32[]{:S(2)}, u32[]{:S(2)}) %collective-permute-start) | collective-permute-done | bytes 163872 | tf_op jit(solution)/shard_map/ppermute | solution.py:69
  45.4 1.6 constant_dynamic-update-slice_fusion.6
  47.0 9.8 %collective-permute-done.1 = bf16[256,320]{0,1:T(8,128)(2,1)} collective-permute-done((bf16[256,320]{0,1:T(8,128)(2,1)S(1)}, bf16[256,320]{0,1:T(8,128)(2,1)}, u32[]{:S(2)}, u32[]{:S(2)}) %collective-permute-start.1) | collective-permute-done | bytes 163872 | tf_op jit(solution)/shard_map/ppermute | solution.py:69
  56.7 1.6 constant_dynamic-update-slice_fusion.5
  58.3 1.6 constant_dynamic-update-slice_fusion.4
  59.9 22.9 %reduce-scatter.7.cloned.1.call-done = bf16[1280,256]{1,0:T(8,128)(2,1)} async-done(((bf16[5120,256]{1,0:T(8,128)(2,1)}), bf16[1280,256]{1,0:T(8,128)(2,1)}) %reduce-scatter.7.cloned.1.call-update) | async-done | bytes 655376 | tf_op jit(solution)/shard_map/reduce_scatter | solution.py:120
  82.8 3.7 %multiply_reduce_fusion.2 = (f32[256]{0:T(256)S(1)}, f32[256]{0:T(256)S(1)}, f32[256]{0:T(256)S(1)}, f32[256]{0:T(256)S(1)}, f32[256]{0:T(256)S(1)}, /*index=5*/...) fusion(f32[1280]{0:T(1024)S(1)} %copy-done.14, bf16[1280,256]{1,0:T(8,128)(2,1)} %reduce-scatter.7.cloned.1.call-done, ...), kind=kOutput, calls=%fused_computation.60 | convolution fusion | flops 843774208 | bytes 5910528 | tf_op jit(solution)/shard_map/dot_general | solution.py:153
  87.2 4.4 %collective-permute-start.3 = (f32[8,256]{1,0:T(8,128)S(1)}, f32[8,256]{1,0:T(8,128)S(1)}, u32[]{:S(2)}, u32[]{:S(2)}) collective-permute-start(f32[8,256]{1,0:T(8,128)S(1)} %stack.55), channel_id=1, source_target_pairs={{0,4},{4,8},{8,12},{12,0},{1,5},{5,9},{9,13},{13,1},{2,6},{6,10},{... | collective-permute-start | bytes 24584 | tf_op jit(solution)/shard_map/ppermute | solution.py:69
  91.6 2.8 %collective-permute-start.5 = (f32[8,256]{1,0:T(8,128)S(1)}, f32[8,256]{1,0:T(8,128)S(1)}, u32[]{:S(2)}, u32[]{:S(2)}) collective-permute-start(f32[8,256]{1,0:T(8,128)S(1)} %stack.55), channel_id=1, source_target_pairs={{0,12},{4,0},{8,4},{12,8},{1,13},{5,1},{9,5},{13,9},{2,14},{6,2},{... | collective-permute-start | bytes 24584 | tf_op jit(solution)/shard_map/ppermute | solution.py:69
  94.5 1.7 collective-permute-done.4
  96.3 1.9 fusion.34
  98.3 2.5 convolution_convert_fusion.4
  100.8 1.2 constant_dynamic-update-slice_fusion.3
  102.8 0.9 collective-permute-start.9
  103.7 2.5 convolution_convert_fusion.5
  106.5 2.5 fusion.4
  109.0 1.5 collective-permute-start.8
  110.5 3.6 %collective-permute-start.10 = (bf16[256,320]{0,1:T(8,128)(2,1)S(1)}, bf16[256,320]{0,1:T(8,128)(2,1)}, u32[]{:S(2)}, u32[]{:S(2)}) collective-permute-start(bf16[256,320]{0,1:T(8,128)(2,1)S(1)} %get-tuple-element.31), channel_id=1, source_target_pairs={{0,8},{4,12},{8,0},{12,4},{1,9},{5,13},{9,1},{13,5},{2,10},{6,14},... | collective-permute-start | bytes 491528 | tf_op jit(solution)/shard_map/ppermute | solution.py:69
  115.4 1.6 constant_dynamic-update-slice_fusion.2
  117.0 11.4 %collective-permute-done.10 = bf16[256,320]{0,1:T(8,128)(2,1)} collective-permute-done((bf16[256,320]{0,1:T(8,128)(2,1)S(1)}, bf16[256,320]{0,1:T(8,128)(2,1)}, u32[]{:S(2)}, u32[]{:S(2)}) %collective-permute-start.10) | collective-permute-done | bytes 163872 | tf_op jit(solution)/shard_map/ppermute | solution.py:69
  128.4 1.6 constant_dynamic-update-slice_fusion.1
  130.0 1.6 collective-permute-done.11
  131.7 1.6 constant_dynamic-update-slice_fusion
  133.3 3.3 %fusion.8 = bf16[1280,256]{1,0:T(8,128)(2,1)} fusion(bf16[1280,256]{1,0:T(8,128)(2,1)} %copy-done.4, bf16[1280,1280]{1,0:T(8,128)(2,1)S(1)} %copy-done), kind=kOutput, calls=%fused_computation.27 | convolution fusion | flops 839188480 | bytes 4587520 | tf_op jit(solution)/shard_map/dot_general | solution.py:162
  136.6 3.0 %fusion.3 = bf16[1280,320]{0,1:T(8,128)(2,1)} fusion(bf16[1280,256]{1,0:T(8,128)(2,1)} %copy-done.4, bf16[1280,320]{0,1:T(8,128)(2,1)} %collective-permute-done.8, bf16[1280,320]{0,1:T(8,128)(2,1)} %collective-permute-done.6, bf16[256,1280]{0,1:T(8,128)(2,1)} %constant_dynamic-update-slice_fusion.4, s32[]{:T(128)S(6)} %select_n.108), kind=kOutput, calls=%fused_computation.18 | convolution fusion | flops 211763200 | bytes 3276804 | tf_op jit(solution)/shard_map/dot_general | solution.py:107
  139.6 18.1 %reduce-scatter.5.cloned.1.call-done = bf16[1536,256]{1,0:T(8,128)(2,1)} async-done(((bf16[6144,256]{1,0:T(8,128)(2,1)}), bf16[1536,256]{1,0:T(8,128)(2,1)}) %reduce-scatter.5.cloned.1.call-update) | async-done | bytes 786448 | tf_op jit(solution)/shard_map/reduce_scatter | solution.py:120
  157.8 5.3 %multiply_reduce_fusion = (f32[256]{0:T(256)S(1)}, f32[256]{0:T(256)S(1)}, f32[256]{0:T(256)S(1)}, f32[256]{0:T(256)S(1)}, f32[256]{0:T(256)S(1)}, /*index=5*/f3...) fusion(f32[1536]{0:T(1024)S(1)} %copy-done.15, bf16[1536,256]{1,0:T(8,128)(2,1)} %reduce-scatter.5.cloned.1.call-done, ...), kind=kOutput, calls=%fused_computation.48 | convolution fusion | flops 1012529408 | bytes 6960128 | tf_op jit(solution)/shard_map/dot_general | solution.py:156
  163.7 4.9 %collective-permute-start.12 = (f32[8,256]{1,0:T(8,128)S(1)}, f32[8,256]{1,0:T(8,128)S(1)}, u32[]{:S(2)}, u32[]{:S(2)}) collective-permute-start(f32[8,256]{1,0:T(8,128)S(1)} %stack.63), channel_id=1, source_target_pairs={{0,4},{4,8},{8,12},{12,0},{1,5},{5,9},{9,13},{13,1},{2,6},{6,10},{... | collective-permute-start | bytes 24584 | tf_op jit(solution)/shard_map/ppermute | solution.py:69
  168.6 2.8 %collective-permute-start.14 = (f32[8,256]{1,0:T(8,128)S(1)}, f32[8,256]{1,0:T(8,128)S(1)}, u32[]{:S(2)}, u32[]{:S(2)}) collective-permute-start(f32[8,256]{1,0:T(8,128)S(1)} %stack.63), channel_id=1, source_target_pairs={{0,12},{4,0},{8,4},{12,8},{1,13},{5,1},{9,5},{13,9},{2,14},{6,2},{... | collective-permute-start | bytes 24584 | tf_op jit(solution)/shard_map/ppermute | solution.py:69
  171.6 1.6 collective-permute-done.13
  173.3 2.3 fusion.24
  175.6 2.5 convolution_convert_fusion.2
  178.1 2.5 fusion.7
  180.7 2.7 convolution_convert_fusion.3
  183.9 2.7 fusion.5
  186.6 6.3 %reduce-scatter.11.cloned.1.call-done = bf16[320,256]{1,0:T(8,128)(2,1)} async-done(((bf16[1280,256]{1,0:T(8,128)(2,1)}), bf16[320,256]{1,0:T(8,128)(2,1)}) %reduce-scatter.11.cloned.1.call-update) | async-done | bytes 163856 | tf_op jit(solution)/shard_map/reduce_scatter | solution.py:166
  192.9 1.2 fusion.46
  194.1 2.0 convolution_convert_fusion.8
  196.0 2.0 convolution_convert_fusion.9
  198.5 2.1 fusion.65
  200.6 15.5 %reduce-scatter.9.cloned.1.call-done = bf16[320,256]{1,0:T(8,128)(2,1)} async-done(((bf16[1280,256]{1,0:T(8,128)(2,1)}), bf16[320,256]{1,0:T(8,128)(2,1)}) %reduce-scatter.9.cloned.1.call-update) | async-done | bytes 163856 | tf_op jit(solution)/shard_map/reduce_scatter | solution.py:174
  216.1 1.2 fusion.40
  217.4 1.8 fusion.109
  219.1 1.0 convolution_convert_fusion.10
  220.2 1.1 fusion.67
  221.3 1.4 fusion.6
  222.7 1.5 collective-permute-start.17
  224.2 1.4 convolution_convert_fusion.11
  226.2 1.4 add_convert_fusion.1
  228.2 1.4 add_convert_fusion.3
  229.6 1.6 collective-permute-start.20
  231.2 21.0 %collective-permute-done.23 = bf16[320,320]{1,0:T(8,128)(2,1)S(1)} collective-permute-done((bf16[320,320]{1,0:T(8,128)(2,1)S(1)}, bf16[320,320]{1,0:T(8,128)(2,1)S(1)}, u32[]{:S(2)}, u32[]{:S(2)}) %collective-permute-start.23) | collective-permute-done | bytes 204832 | tf_op jit(solution)/shard_map/ppermute | solution.py:114
  252.2 1.7 add_convert_fusion
  253.9 0.9 collective-permute-done.20
  255.6 2.8 %fusion.2 = bf16[1536,320]{0,1:T(8,128)(2,1)} fusion(bf16[1536,256]{1,0:T(8,128)(2,1)S(1)} %copy-done.3, bf16[1536,320]{0,1:T(8,128)(2,1)S(1)} %collective-permute-done.17, bf16[1536,320]{0,1:T(8,128)(2,1)} %collective-permute-done.15, bf16[256,1280]{0,1:T(8,128)(2,1)} %constant_dynamic-update-slice_fusion, s32[]{:T(128)S(6)} %select_n.108), kind=kOutput, calls=%fused_computation.15 | convolution fusion | flops 254115840 | bytes 3899396 | tf_op jit(solution)/shard_map/dot_general | solution.py:107
  258.4 3.9 %all-reduce.2.cloned.1.call-done = bf16[256,1280]{1,0:T(8,128)(2,1)} async-done(((bf16[256,1280]{1,0:T(8,128)(2,1)}), bf16[256,1280]{1,0:T(8,128)(2,1)}) %all-reduce.2.cloned.1.call-update) | async-done | bytes 655376 | tf_op jit(solution)/shard_map/psum | solution.py:186
  262.3 2.0 copy.47
  (96 shorter events, 8.0 us)
Async XLA Ops:
  7.2 75.7 %copy-start = (bf16[1280,1280]{1,0:T(8,128)(2,1)S(1)}, bf16[1280,1280]{1,0:T(8,128)(2,1)}, u32[]{:S(2)}) copy-start(bf16[1280,1280]{1,0:T(8,128)(2,1)} %param.21) | copy-start | bytes 9830404
  7.2 75.6 %reduce-scatter.7.cloned.1.call-start = ((), (), s32[]{:S(2)}) async-start(), calls=%async_computation.5 | async-start | bytes 3276800 | tf_op jit(solution)/shard_map/reduce_scatter | solution.py:120
  17.5 140.3 %reduce-scatter.5.cloned.1.call-start = ((), (), s32[]{:S(2)}) async-start(), calls=%async_computation.4 | async-start | bytes 3932160 | tf_op jit(solution)/shard_map/reduce_scatter | solution.py:120
  28.2 10.5 %copy-start.14 = (f32[1280]{0:T(1024)S(1)}, f32[1280]{0:T(1024)}, u32[]{:S(2)}) copy-start(f32[1280]{0:T(1024)} %param.16) | copy-start | bytes 15364
  28.2 164.7 %reduce-scatter.11.cloned.1.call-start = ((), (), s32[]{:S(2)}) async-start(), calls=%async_computation.7 | async-start | bytes 819200 | tf_op jit(solution)/shard_map/reduce_scatter | solution.py:166
  31.7 13.7 %collective-permute-start = (bf16[256,320]{0,1:T(8,128)(2,1)S(1)}, bf16[256,320]{0,1:T(8,128)(2,1)}, u32[]{:S(2)}, u32[]{:S(2)}) collective-permute-start(bf16[256,320]{0,1:T(8,128)(2,1)S(1)} %get-tuple-element.36), channel_id=1, source_target_pairs={{0,4},{4,8},{8,12},{12,0},{1,5},{5,9},{9,13},{13,1},{2,6},{6,10},{... | collective-permute-start | bytes 491528 | tf_op jit(solution)/shard_map/ppermute | solution.py:69
  34.7 22.0 %collective-permute-start.1 = (bf16[256,320]{0,1:T(8,128)(2,1)S(1)}, bf16[256,320]{0,1:T(8,128)(2,1)}, u32[]{:S(2)}, u32[]{:S(2)}) collective-permute-start(bf16[256,320]{0,1:T(8,128)(2,1)S(1)} %get-tuple-element.36), channel_id=1, source_target_pairs={{0,8},{4,12},{8,0},{12,4},{1,9},{5,13},{9,1},{13,5},{2,10},{6,14},... | collective-permute-start | bytes 491528 | tf_op jit(solution)/shard_map/ppermute | solution.py:69
  37.3 21.0 %collective-permute-start.2 = (bf16[256,320]{0,1:T(8,128)(2,1)S(1)}, bf16[256,320]{0,1:T(8,128)(2,1)}, u32[]{:S(2)}, u32[]{:S(2)}) collective-permute-start(bf16[256,320]{0,1:T(8,128)(2,1)S(1)} %get-tuple-element.36), channel_id=1, source_target_pairs={{0,12},{4,0},{8,4},{12,8},{1,13},{5,1},{9,5},{13,9},{2,14},{6,2},{... | collective-permute-start | bytes 491528 | tf_op jit(solution)/shard_map/ppermute | solution.py:69
  87.2 7.3 %collective-permute-start.3 = (f32[8,256]{1,0:T(8,128)S(1)}, f32[8,256]{1,0:T(8,128)S(1)}, u32[]{:S(2)}, u32[]{:S(2)}) collective-permute-start(f32[8,256]{1,0:T(8,128)S(1)} %stack.55), channel_id=1, source_target_pairs={{0,4},{4,8},{8,12},{12,0},{1,5},{5,9},{9,13},{13,1},{2,6},{6,10},{... | collective-permute-start | bytes 24584 | tf_op jit(solution)/shard_map/ppermute | solution.py:69
  91.6 4.7 %collective-permute-start.4 = (f32[8,256]{1,0:T(8,128)S(1)}, f32[8,256]{1,0:T(8,128)S(1)}, u32[]{:S(2)}, u32[]{:S(2)}) collective-permute-start(f32[8,256]{1,0:T(8,128)S(1)} %stack.55), channel_id=1, source_target_pairs={{0,8},{4,12},{8,0},{12,4},{1,9},{5,13},{9,1},{13,5},{2,10},{6,14},... | collective-permute-start | bytes 24584 | tf_op jit(solution)/shard_map/ppermute | solution.py:69
  91.6 4.6 %collective-permute-start.5 = (f32[8,256]{1,0:T(8,128)S(1)}, f32[8,256]{1,0:T(8,128)S(1)}, u32[]{:S(2)}, u32[]{:S(2)}) collective-permute-start(f32[8,256]{1,0:T(8,128)S(1)} %stack.55), channel_id=1, source_target_pairs={{0,12},{4,0},{8,4},{12,8},{1,13},{5,1},{9,5},{13,9},{2,14},{6,2},{... | collective-permute-start | bytes 24584 | tf_op jit(solution)/shard_map/ppermute | solution.py:69
  98.2 3.8 %copy-start.4 = (bf16[1280,256]{1,0:T(8,128)(2,1)}, bf16[1280,256]{1,0:T(8,128)(2,1)S(1)}, u32[]{:S(2)}) copy-start(bf16[1280,256]{1,0:T(8,128)(2,1)S(1)} %fusion.34) | copy-start | bytes 1966084
  98.2 2.6 copy-start.6
  98.3 2.6 copy-start.9
  100.7 5.7 %collective-permute-start.7 = (bf16[1280,320]{0,1:T(8,128)(2,1)}, bf16[1280,320]{0,1:T(8,128)(2,1)}, u32[]{:S(2)}, u32[]{:S(2)}) collective-permute-start(bf16[1280,320]{0,1:T(8,128)(2,1)} %convolution_convert_fusion.4), channel_id=1, source_target_pairs={{0,1},{1,0},{2,3},{3,2},{4,5},{5,4},{6,7},{7,6},{8,9},{9,8},{10,11... | collective-permute-start | bytes 2457608 | tf_op jit(solution)/shard_map/ppermute | solution.py:109
  102.0 0.8 copy-start.11
  102.8 12.6 %collective-permute-start.9 = (bf16[256,320]{0,1:T(8,128)(2,1)S(1)}, bf16[256,320]{0,1:T(8,128)(2,1)}, u32[]{:S(2)}, u32[]{:S(2)}) collective-permute-start(bf16[256,320]{0,1:T(8,128)(2,1)S(1)} %get-tuple-element.31), channel_id=1, source_target_pairs={{0,4},{4,8},{8,12},{12,0},{1,5},{5,9},{9,13},{13,1},{2,6},{6,10},{... | collective-permute-start | bytes 491528 | tf_op jit(solution)/shard_map/ppermute | solution.py:69
  103.7 2.8 %copy-start.5 = (bf16[1280,256]{1,0:T(8,128)(2,1)S(1)}, bf16[1280,256]{1,0:T(8,128)(2,1)}, u32[]{:S(2)}) copy-start(bf16[1280,256]{1,0:T(8,128)(2,1)} %copy-done.4) | copy-start | bytes 1966084
  106.2 8.2 %copy-start.15 = (f32[1536]{0:T(1024)S(1)}, f32[1536]{0:T(1024)}, u32[]{:S(2)}) copy-start(f32[1536]{0:T(1024)} %param.15) | copy-start | bytes 18436
  106.2 30.4 %collective-permute-start.6 = (bf16[1280,320]{0,1:T(8,128)(2,1)}, bf16[1280,320]{0,1:T(8,128)(2,1)}, u32[]{:S(2)}, u32[]{:S(2)}) collective-permute-start(bf16[1280,320]{0,1:T(8,128)(2,1)} %convolution_convert_fusion.5), channel_id=1, source_target_pairs={{0,1},{1,0},{2,3},{3,2},{4,5},{5,4},{6,7},{7,6},{8,9},{9,8},{10,11... | collective-permute-start | bytes 2457608 | tf_op jit(solution)/shard_map/ppermute | solution.py:110
  109.0 27.6 %collective-permute-start.8 = (bf16[1280,320]{0,1:T(8,128)(2,1)}, bf16[1280,320]{0,1:T(8,128)(2,1)}, u32[]{:S(2)}, u32[]{:S(2)}) collective-permute-start(bf16[1280,320]{0,1:T(8,128)(2,1)} %fusion.4), channel_id=1, source_target_pairs={{0,2},{2,0},{1,3},{3,1},{4,6},{6,4},{5,7},{7,5},{8,10},{10,8},{9,1... | collective-permute-start | bytes 2457608 | tf_op jit(solution)/shard_map/ppermute | solution.py:114
  110.5 18.0 %collective-permute-start.10 = (bf16[256,320]{0,1:T(8,128)(2,1)S(1)}, bf16[256,320]{0,1:T(8,128)(2,1)}, u32[]{:S(2)}, u32[]{:S(2)}) collective-permute-start(bf16[256,320]{0,1:T(8,128)(2,1)S(1)} %get-tuple-element.31), channel_id=1, source_target_pairs={{0,8},{4,12},{8,0},{12,4},{1,9},{5,13},{9,1},{13,5},{2,10},{6,14},... | collective-permute-start | bytes 491528 | tf_op jit(solution)/shard_map/ppermute | solution.py:69
  114.1 17.6 %collective-permute-start.11 = (bf16[256,320]{0,1:T(8,128)(2,1)S(1)}, bf16[256,320]{0,1:T(8,128)(2,1)}, u32[]{:S(2)}, u32[]{:S(2)}) collective-permute-start(bf16[256,320]{0,1:T(8,128)(2,1)S(1)} %get-tuple-element.31), channel_id=1, source_target_pairs={{0,12},{4,0},{8,4},{12,8},{1,13},{5,1},{9,5},{13,9},{2,14},{6,2},{... | collective-permute-start | bytes 491528 | tf_op jit(solution)/shard_map/ppermute | solution.py:69
  163.7 7.8 %collective-permute-start.12 = (f32[8,256]{1,0:T(8,128)S(1)}, f32[8,256]{1,0:T(8,128)S(1)}, u32[]{:S(2)}, u32[]{:S(2)}) collective-permute-start(f32[8,256]{1,0:T(8,128)S(1)} %stack.63), channel_id=1, source_target_pairs={{0,4},{4,8},{8,12},{12,0},{1,5},{5,9},{9,13},{13,1},{2,6},{6,10},{... | collective-permute-start | bytes 24584 | tf_op jit(solution)/shard_map/ppermute | solution.py:69
  168.6 4.5 %collective-permute-start.13 = (f32[8,256]{1,0:T(8,128)S(1)}, f32[8,256]{1,0:T(8,128)S(1)}, u32[]{:S(2)}, u32[]{:S(2)}) collective-permute-start(f32[8,256]{1,0:T(8,128)S(1)} %stack.63), channel_id=1, source_target_pairs={{0,8},{4,12},{8,0},{12,4},{1,9},{5,13},{9,1},{13,5},{2,10},{6,14},... | collective-permute-start | bytes 24584 | tf_op jit(solution)/shard_map/ppermute | solution.py:69
  168.6 4.6 %collective-permute-start.14 = (f32[8,256]{1,0:T(8,128)S(1)}, f32[8,256]{1,0:T(8,128)S(1)}, u32[]{:S(2)}, u32[]{:S(2)}) collective-permute-start(f32[8,256]{1,0:T(8,128)S(1)} %stack.63), channel_id=1, source_target_pairs={{0,12},{4,0},{8,4},{12,8},{1,13},{5,1},{9,5},{13,9},{2,14},{6,2},{... | collective-permute-start | bytes 24584 | tf_op jit(solution)/shard_map/ppermute | solution.py:69
  171.5 44.6 %reduce-scatter.9.cloned.1.call-start = ((), (), s32[]{:S(2)}) async-start(), calls=%async_computation.6 | async-start | bytes 819200 | tf_op jit(solution)/shard_map/reduce_scatter | solution.py:174
  173.3 4.8 %copy-start.16 = (bf16[1536,1280]{1,0:T(8,128)(2,1)S(1)}, bf16[1536,1280]{1,0:T(8,128)(2,1)}, u32[]{:S(2)}) copy-start(bf16[1536,1280]{1,0:T(8,128)(2,1)} %param.20) | copy-start | bytes 11796484
  175.5 2.5 copy-start.1
  178.1 5.8 %collective-permute-start.16 = (bf16[1536,320]{0,1:T(8,128)(2,1)}, bf16[1536,320]{0,1:T(8,128)(2,1)}, u32[]{:S(2)}, u32[]{:S(2)}) collective-permute-start(bf16[1536,320]{0,1:T(8,128)(2,1)} %convolution_convert_fusion.2), channel_id=1, source_target_pairs={{0,1},{1,0},{2,3},{3,2},{4,5},{5,4},{6,7},{7,6},{8,9},{9,8},{10,11... | collective-permute-start | bytes 2949128 | tf_op jit(solution)/shard_map/ppermute | solution.py:109
  180.6 81.6 %all-reduce.2.cloned.1.call-start = ((), (), s32[]{:S(2)}) async-start(), calls=%async_computation.8 | async-start | bytes 1310720 | tf_op jit(solution)/shard_map/psum | solution.py:186
  180.7 3.2 %copy-start.2 = (bf16[1536,256]{1,0:T(8,128)(2,1)S(1)}, bf16[1536,256]{1,0:T(8,128)(2,1)}, u32[]{:S(2)}) copy-start(bf16[1536,256]{1,0:T(8,128)(2,1)} %copy-done.1) | copy-start | bytes 2359300
  183.4 72.2 %collective-permute-start.15 = (bf16[1536,320]{0,1:T(8,128)(2,1)}, bf16[1536,320]{0,1:T(8,128)(2,1)}, u32[]{:S(2)}, u32[]{:S(2)}) collective-permute-start(bf16[1536,320]{0,1:T(8,128)(2,1)} %convolution_convert_fusion.3), channel_id=1, source_target_pairs={{0,1},{1,0},{2,3},{3,2},{4,5},{5,4},{6,7},{7,6},{8,9},{9,8},{10,11... | collective-permute-start | bytes 2949128 | tf_op jit(solution)/shard_map/ppermute | solution.py:110
  196.0 29.6 %collective-permute-start.22 = (bf16[320,320]{1,0:T(8,128)(2,1)}, bf16[320,320]{1,0:T(8,128)(2,1)}, u32[]{:S(2)}, u32[]{:S(2)}) collective-permute-start(bf16[320,320]{1,0:T(8,128)(2,1)} %convolution_convert_fusion.8), channel_id=1, source_target_pairs={{0,1},{1,0},{2,3},{3,2},{4,5},{5,4},{6,7},{7,6},{8,9},{9,8},{10,11... | collective-permute-start | bytes 614408 | tf_op jit(solution)/shard_map/ppermute | solution.py:109
  198.0 31.5 %collective-permute-start.21 = (bf16[320,320]{1,0:T(8,128)(2,1)}, bf16[320,320]{1,0:T(8,128)(2,1)}, u32[]{:S(2)}, u32[]{:S(2)}) collective-permute-start(bf16[320,320]{1,0:T(8,128)(2,1)} %convolution_convert_fusion.9), channel_id=1, source_target_pairs={{0,1},{1,0},{2,3},{3,2},{4,5},{5,4},{6,7},{7,6},{8,9},{9,8},{10,11... | collective-permute-start | bytes 614408 | tf_op jit(solution)/shard_map/ppermute | solution.py:110
  216.1 3.0 %copy-start.7 = (bf16[256,1280]{1,0:T(8,128)(2,1)S(1)}, bf16[256,1280]{1,0:T(8,128)(2,1)}, u32[]{:S(2)}) copy-start(bf16[256,1280]{1,0:T(8,128)(2,1)} %param.17) | copy-start | bytes 1966084
  217.4 2.8 %copy-start.8 = (bf16[320,256]{1,0:T(8,128)(2,1)}, bf16[320,256]{1,0:T(8,128)(2,1)S(1)}, u32[]{:S(2)}) copy-start(bf16[320,256]{1,0:T(8,128)(2,1)S(1)} %fusion.40) | copy-start | bytes 491524
  217.4 3.9 %copy-start.10 = (bf16[320,1280]{1,0:T(8,128)(2,1)S(1)}, bf16[320,1280]{1,0:T(8,128)(2,1)}, u32[]{:S(2)}) copy-start(bf16[320,1280]{1,0:T(8,128)(2,1)} %param.19) | copy-start | bytes 2457604
  222.7 29.5 %copy-start.12 = (f32[320,320]{1,0:T(8,128)S(1)}, f32[320,320]{1,0:T(8,128)}, u32[]{:S(2)}) copy-start(f32[320,320]{1,0:T(8,128)} %fusion.65) | copy-start | bytes 1228804
  222.7 32.9 %collective-permute-start.17 = (bf16[1536,320]{0,1:T(8,128)(2,1)}, bf16[1536,320]{0,1:T(8,128)(2,1)S(1)}, u32[]{:S(2)}, u32[]{:S(2)}) collective-permute-start(bf16[1536,320]{0,1:T(8,128)(2,1)} %fusion.5), channel_id=1, source_target_pairs={{0,2},{2,0},{1,3},{3,1},{4,6},{6,4},{5,7},{7,5},{8,10},{10,8},{9,1... | collective-permute-start | bytes 2949128 | tf_op jit(solution)/shard_map/ppermute | solution.py:114
  224.2 3.4 %collective-permute-start.19 = (bf16[320,320]{1,0:T(8,128)(2,1)}, bf16[320,320]{1,0:T(8,128)(2,1)S(1)}, u32[]{:S(2)}, u32[]{:S(2)}) collective-permute-start(bf16[320,320]{1,0:T(8,128)(2,1)} %convolution_convert_fusion.10), channel_id=1, source_target_pairs={{0,1},{1,0},{2,3},{3,2},{4,5},{5,4},{6,7},{7,6},{8,9},{9,8},{10,11... | collective-permute-start | bytes 614408 | tf_op jit(solution)/shard_map/ppermute | solution.py:109
  225.6 29.2 %copy-start.13 = (f32[320,320]{1,0:T(8,128)S(1)}, f32[320,320]{1,0:T(8,128)}, u32[]{:S(2)}) copy-start(f32[320,320]{1,0:T(8,128)} %fusion.67) | copy-start | bytes 1228804
  225.6 28.3 %collective-permute-start.18 = (bf16[320,320]{1,0:T(8,128)(2,1)S(1)}, bf16[320,320]{1,0:T(8,128)(2,1)S(1)}, u32[]{:S(2)}, u32[]{:S(2)}) collective-permute-start(bf16[320,320]{1,0:T(8,128)(2,1)S(1)} %convolution_convert_fusion.11), channel_id=1, source_target_pairs={{0,1},{1,0},{2,3},{3,2},{4,5},{5,4},{6,7},{7,6},{8,9},{9,8},{10,11... | collective-permute-start | bytes 614408 | tf_op jit(solution)/shard_map/ppermute | solution.py:110
  227.6 27.9 %copy-start.3 = (bf16[1536,256]{1,0:T(8,128)(2,1)S(1)}, bf16[1536,256]{1,0:T(8,128)(2,1)}, u32[]{:S(2)}) copy-start(bf16[1536,256]{1,0:T(8,128)(2,1)} %copy-done.1) | copy-start | bytes 2359300
  227.6 24.5 %collective-permute-start.23 = (bf16[320,320]{1,0:T(8,128)(2,1)S(1)}, bf16[320,320]{1,0:T(8,128)(2,1)S(1)}, u32[]{:S(2)}, u32[]{:S(2)}) collective-permute-start(bf16[320,320]{1,0:T(8,128)(2,1)S(1)} %add_convert_fusion.1), channel_id=1, source_target_pairs={{0,2},{2,0},{1,3},{3,1},{4,6},{6,4},{5,7},{7,5},{8,10},{10,8},{9,1... | collective-permute-start | bytes 614408 | tf_op jit(solution)/shard_map/ppermute | solution.py:114
  229.6 25.2 %collective-permute-start.20 = (bf16[320,320]{1,0:T(8,128)(2,1)S(1)}, bf16[320,320]{1,0:T(8,128)(2,1)S(1)}, u32[]{:S(2)}, u32[]{:S(2)}) collective-permute-start(bf16[320,320]{1,0:T(8,128)(2,1)S(1)} %add_convert_fusion.3), channel_id=1, source_target_pairs={{0,2},{2,0},{1,3},{3,1},{4,6},{6,4},{5,7},{7,5},{8,10},{10,8},{9,1... | collective-permute-start | bytes 614408 | tf_op jit(solution)/shard_map/ppermute | solution.py:114
Sparse Core Ops, SparseCore 0:
  17.6 65.1 reduce-scatter.6
  85.1 72.5 reduce-scatter.4
  171.6 21.2 reduce-scatter.10
  195.1 21.0 reduce-scatter.8
  222.8 39.4 all-reduce.1
